TPU v7x, 128 devices: a whole 4x4x4 slice. The times are simulated.
128 devices in a mesh: dp: 32 (over y, z, core), mp: 4 (over x).
Axes of the slice: x: 4, y: 4, z: 4, core: 2. Of those that a mesh axis runs over, the one named last changes fastest.
Arguments:
- layer_in: bfloat16 [8192, 2048], P('dp'), may hold values from -6 to 6
- cotangent: bfloat16 [8192, 2048], P('dp', 'mp'), may hold values from -6 to 6
- segments: int32 [8192], P('dp'), may hold values from 0 to 7, as said below
- adapters: int32 [8], replicated, may hold values from 0 to 7
- norm_one: float32 [2048], replicated, may hold values from 0.5 to 1.5
- norm_two: float32 [2048], replicated, may hold values from 0.5 to 1.5
- out_gain: float32 [128], replicated, may hold values from 0.5 to 1.5
- beta_bias: float32 [16], P('mp'), may hold values from -7.5 to 0
- conv_taps: bfloat16 [4, 3, 2048], P(None, None, 'mp'), may hold values from -3 to 3
- w_qkv: bfloat16 [2048, 3, 2048], P('dp', None, 'mp'), may hold values from -0.125 to 0.125
- w_beta: bfloat16 [2048, 16], P('dp', 'mp'), may hold values from -0.125 to 0.125
- w_out: bfloat16 [2048, 2048], P('mp', 'dp'), may hold values from -0.125 to 0.125
- w_gate_up: bfloat16 [2048, 2, 5632], P('dp', None, 'mp'), may hold values from -0.125 to 0.125
- w_down: bfloat16 [5632, 2048], P('mp', 'dp'), may hold values from -0.078125 to 0.078125
- a_in: bfloat16 [2048, 6, 128], P(('dp', 'mp')), may hold values from -0.125 to 0.125
- b_heads: bfloat16 [3, 128, 2048], P(None, 'dp', 'mp'), may hold values from -0.75 to 0.75
- b_beta: bfloat16 [128, 16], P('dp', 'mp'), may hold values from -0.75 to 0.75
- a_out: bfloat16 [2048, 128], P('mp', 'dp'), may hold values from -0.125 to 0.125
- b_ffn: bfloat16 [2, 128, 5632], P(None, 'dp', 'mp'), may hold values from -0.75 to 0.75
- a_down: bfloat16 [5632, 128], P('mp', 'dp'), may hold values from -0.078125 to 0.078125
- b_res: bfloat16 [2, 128, 2048], P(None, None, ('dp', 'mp')), may hold values from -0.75 to 0.75
Outputs:
- output: bfloat16 [8192, 2048], P('dp', 'mp')
- grad_input: float32 [8192, 2048], P('dp', 'mp')
- grad_a_in: float32 [2048, 6, 128], P(('dp', 'mp'))
- grad_b_heads: float32 [3, 128, 2048], P(None, 'dp', 'mp')
- grad_b_beta: float32 [128, 16], P('dp', 'mp')
- grad_a_out: float32 [2048, 128], P('mp', 'dp')
- grad_b_ffn: float32 [2, 128, 5632], P(None, 'dp', 'mp')
- grad_a_down: float32 [5632, 128], P('mp', 'dp')
- grad_b_res: float32 [2, 128, 2048], P(None, None, ('dp', 'mp'))
Inputs may be any that keep to these rules, and one draw needn't show every extreme that they name: `segments`: document numbers start at 0, never fall, and rise by one at every multiple of 8192 tokens and at 7 further places inside each packed sequence, never at the first token of an index of dp and one of them within the first 256 tokens of the sequence; a packed sequence spans 32 indices of dp.
All inputs are finite; a program needn't handle non-finite values.
Results may differ from a plain program's by a relative error of at most 0.03.
Values may be sent and summed in bfloat16 or wider, within the bound.
A program may use at most 256 MiB of HBM per device.

v0:
```python
import jax
import jax.numpy as jnp
from jax import lax
from jax.sharding import PartitionSpec as P

DH = 128
KW = 4
BLOCK = 64
RANK = 16


EXACT_PRECISION = lax.Precision.HIGHEST
EPSILON = 1e-06
WIDE = jnp.float32
NARROW = jnp.bfloat16


def from_behind(value, axis, steps):
    count = lax.axis_size(axis)
    leading, last = (max(0, -steps), min(count, count - steps))
    return lax.ppermute(value, axis, [(source, source + steps) for source in range(leading, last)])


def entering(value, axis, join, neutral):
    count, mine = (lax.axis_size(axis), lax.axis_index(axis))
    pieces = jax.tree.map(lambda part: lax.all_gather(part, axis), value)
    so_far = jax.tree.map(
        lambda part, zero: jnp.full_like(part, 0) + jnp.asarray(zero, part.dtype), value, neutral
    )

    def entering_step(position, so_far):
        longer = join(so_far, jax.tree.map(lambda part: part[position], pieces))
        return jax.tree.map(lambda new, old: jnp.where(position < mine, new, old), longer, so_far)

    return lax.fori_loop(0, count - 1, entering_step, so_far)


def prefix(value, axis, combine, identity):
    peers, here = (lax.axis_size(axis), lax.axis_index(axis))
    everything = jax.tree.map(
        lambda part, kind: lax.all_gather(part.astype(kind), axis),
        value,
        jax.tree.map(lambda a: jnp.bfloat16 if a.dtype == jnp.float32 else a.dtype, value),
    )
    start = jax.tree.map(
        lambda part, zero: jnp.broadcast_to(jnp.asarray(zero, part.dtype), part.shape),
        value,
        identity,
    )

    def prefix_step(k, before):
        at = peers - 1 - k
        reached = at > here
        new = combine(
            before, jax.tree.map(lambda part, own: part[at].astype(own.dtype), everything, value)
        )
        return jax.tree.map(lambda a, b: jnp.where(reached, a, b), new, before)

    return lax.fori_loop(0, peers, prefix_step, start)


def inverse_rms(values):
    return lax.rsqrt(jnp.mean(values * values, axis=-1, keepdims=True) + EPSILON)


def unit_rows(values):
    return values * lax.rsqrt(jnp.sum(values * values, axis=-1, keepdims=True) + EPSILON)


def norm_back(values, scale, gain, grad_out):
    weighted = grad_out * gain
    return scale * weighted - values * scale**3 * jnp.mean(
        weighted * values, axis=-1, keepdims=True
    )


def fast_dot(left, right):
    return jnp.dot(left, right, preferred_element_type=WIDE)


def precise_dot(left, right):
    return jnp.dot(left, right, precision=EXACT_PRECISION)


def compose(earlier, later):
    return (
        jnp.einsum("hij,hjk->hik", later[0], earlier[0], precision=EXACT_PRECISION),
        later[1] + jnp.einsum("hij,hjk->hik", later[0], earlier[1], precision=EXACT_PRECISION),
    )


def mixer_core(pre_ext, strength, taps_wide, seg_ext, segments):
    row_count = segments.shape[0]
    summed = jnp.zeros((row_count,) + pre_ext.shape[1:], WIDE)
    for tap_index in range(KW):
        offset = KW - 1 - tap_index
        same_seg = (seg_ext[offset : offset + row_count] == segments).astype(WIDE)
        summed = (
            summed
            + taps_wide[tap_index] * pre_ext[offset : offset + row_count] * same_seg[:, None, None]
        )
    activated = jax.nn.silu(summed)
    heads_local = activated.shape[2] // DH
    queries = unit_rows(activated[:, 0].reshape(row_count, heads_local, DH))
    key_rows = unit_rows(activated[:, 1].reshape(row_count, heads_local, DH))
    value_rows = activated[:, 2].reshape(row_count, heads_local, DH)
    block_count = row_count // BLOCK

    def blocked(tensor):
        return tensor.reshape((block_count, BLOCK) + tensor.shape[1:])

    before_ids = seg_ext[KW - 2 : KW - 2 + row_count].reshape(block_count, BLOCK)[:, 0]
    identity_maps = jnp.broadcast_to(jnp.eye(DH, dtype=WIDE), (heads_local, DH, DH))
    below_ones = jnp.tril(jnp.ones((BLOCK, BLOCK), WIDE), -1)
    upto_ones = jnp.tril(jnp.ones((BLOCK, BLOCK), WIDE), 0)

    def piece_step(carried_pair, block_inputs):
        running_memory_state, accumulated = carried_pair
        q_block, k_block, v_block, b_block, s_block, p_block = block_inputs
        same_seg = (s_block[:, None] == s_block[None, :]).astype(WIDE)
        linked = (s_block == p_block).astype(WIDE)
        q_heads = q_block.transpose(1, 0, 2)
        k_heads = k_block.transpose(1, 0, 2)
        v_heads = v_block.transpose(1, 0, 2)
        b_heads_now = b_block.T
        key_gram = jnp.einsum("hcd,hed->hce", k_heads, k_heads, precision=EXACT_PRECISION)
        lower_part = key_gram * (same_seg * below_ones)[None] * b_heads_now[:, :, None]
        right_side = (
            jnp.concatenate([v_heads, k_heads * linked[None, :, None]], axis=-1)
            * b_heads_now[:, :, None]
        )
        solved = lax.linalg.triangular_solve(
            lower_part, right_side, left_side=True, lower=True, unit_diagonal=True
        )
        initial_write_value = solved[..., :DH]
        dispersal_matrix = solved[..., DH:]
        query_key = (
            jnp.einsum("hcd,hed->hce", q_heads, k_heads, precision=EXACT_PRECISION)
            * (same_seg * upto_ones)[None]
        )
        written_value_rows = initial_write_value - jnp.einsum(
            "sud,sda->sua", dispersal_matrix, running_memory_state, precision=EXACT_PRECISION
        )
        linked_query_rows = q_heads * linked[None, :, None]
        out_block = jnp.einsum(
            "hce,hev->hcv", query_key, written_value_rows, precision=EXACT_PRECISION
        ) + jnp.einsum(
            "sud,sda->sua", linked_query_rows, running_memory_state, precision=EXACT_PRECISION
        )
        reach_map = linked_query_rows - jnp.einsum(
            "hce,hek->hck", query_key, dispersal_matrix, precision=EXACT_PRECISION
        )
        carried_rows = jnp.einsum("hck,hkj->hcj", reach_map, accumulated, precision=EXACT_PRECISION)
        trailing_key_rows = k_heads * same_seg[-1][None, :, None]
        memory_next = linked[-1] * running_memory_state + jnp.einsum(
            "ade,adt->aet", trailing_key_rows, written_value_rows, precision=EXACT_PRECISION
        )
        step_map = linked[-1] * identity_maps - jnp.einsum(
            "hck,hcj->hkj", trailing_key_rows, dispersal_matrix, precision=EXACT_PRECISION
        )
        accumulated_next = jnp.einsum(
            "hkj,hji->hki", step_map, accumulated, precision=EXACT_PRECISION
        )
        return ((memory_next, accumulated_next), (out_block, carried_rows))

    start_pair = (jnp.zeros((heads_local, DH, DH), WIDE), identity_maps)
    scanned = (
        blocked(queries),
        blocked(key_rows),
        blocked(value_rows),
        blocked(strength),
        blocked(segments),
        before_ids,
    )
    (memory_end, map_end), (out_blocks, carried_blocks) = lax.scan(piece_step, start_pair, scanned)
    initial_output_term = out_blocks.transpose(0, 2, 1, 3).reshape(row_count, heads_local, DH)
    carried_state_rows = carried_blocks.transpose(0, 2, 1, 3).reshape(row_count, heads_local, DH)
    return (initial_output_term, carried_state_rows, map_end, memory_end)


def fetch_weights(
    w_qkv, w_beta, w_out, w_gate_up, w_down, a_in, b_heads, b_beta, a_out, b_ffn, a_down, b_res
):
    mixer_parts = (
        lax.all_gather(w_qkv, "dp", axis=0, tiled=True),
        lax.all_gather(w_beta, "dp", axis=0, tiled=True),
        lax.all_gather(w_out, "dp", axis=1, tiled=True),
        lax.all_gather(b_heads, "dp", axis=1, tiled=True),
        lax.all_gather(b_beta, "dp", axis=0, tiled=True),
        lax.all_gather(a_out, "dp", axis=1, tiled=True),
    )
    ffn_parts = (
        lax.all_gather(w_gate_up, "dp", axis=0, tiled=True),
        lax.all_gather(w_down, "dp", axis=1, tiled=True),
        lax.all_gather(b_ffn, "dp", axis=1, tiled=True),
        lax.all_gather(a_down, "dp", axis=1, tiled=True),
    )
    shared_parts = (
        lax.all_gather(a_in, ("dp", "mp"), axis=0, tiled=True),
        lax.all_gather(b_res, ("dp", "mp"), axis=2, tiled=True),
    )
    return tuple(mixer_parts) + tuple(ffn_parts) + tuple(shared_parts)


def forward_pass(
    layer_in, segments, adapter_picks, norm_one, norm_two, out_gain, beta_bias, conv_taps, weights
):
    w_qkv, w_beta, w_out, b_heads, b_beta, a_out, w_gate_up, w_down, b_ffn, a_down, a_in, b_res = (
        weights
    )
    row_count = layer_in.shape[0]
    input_wide = layer_in.astype(WIDE)
    scale_one = inverse_rms(input_wide)
    xn_one = (input_wide * scale_one * norm_one).astype(NARROW)
    u_one = (
        jnp.einsum("td,djr->tjr", xn_one, a_in[:, :4], preferred_element_type=WIDE)
        * adapter_picks[:, None, :]
    ).astype(NARROW)
    projected = jnp.einsum("td,djc->tjc", xn_one, w_qkv, preferred_element_type=WIDE) + jnp.einsum(
        "tjr,jrc->tjc", u_one[:, :3], b_heads, preferred_element_type=WIDE
    )
    pre_conv = projected.astype(NARROW)
    strength = jax.nn.sigmoid(fast_dot(xn_one, w_beta) + fast_dot(u_one[:, 3], b_beta) + beta_bias)
    edge_rows, edge_ids = from_behind(
        (pre_conv[row_count - KW + 1 :], (segments[row_count - KW + 1 :] + 1).astype(NARROW)),
        "dp",
        1,
    )
    seg_ext = jnp.concatenate([edge_ids.astype(jnp.int32) - 1, segments])
    pre_ext = jnp.concatenate([edge_rows, pre_conv]).astype(WIDE)
    taps_wide = conv_taps.astype(WIDE)
    core_outputs, core_back = jax.vjp(
        lambda pre_in, strength_in: mixer_core(pre_in, strength_in, taps_wide, seg_ext, segments),
        pre_ext,
        strength,
    )
    initial_output_term, carried_state_rows, trans_map, offset_map = core_outputs
    identity_maps = jnp.broadcast_to(jnp.eye(DH, dtype=WIDE), trans_map.shape)
    incoming = entering(
        (trans_map, offset_map), "dp", compose, (identity_maps, jnp.zeros_like(offset_map))
    )
    incoming_state_value = incoming[1]
    mixer_output_rows = initial_output_term + jnp.einsum(
        "gox,oxj->goj", carried_state_rows, incoming_state_value, precision=EXACT_PRECISION
    )
    mixer_scale = inverse_rms(mixer_output_rows)
    normed = (mixer_output_rows * mixer_scale * out_gain).astype(NARROW).reshape(row_count, -1)
    u_out = fast_dot(normed, a_out) * adapter_picks
    partial_mix = fast_dot(normed, w_out) + precise_dot(u_out, b_res[0].astype(WIDE))
    branch = lax.psum(partial_mix, "mp")
    hidden_one = input_wide + branch
    scale_two = inverse_rms(hidden_one)
    xn_two = (hidden_one * scale_two * norm_two).astype(NARROW)
    u_two = (
        jnp.einsum("td,djr->tjr", xn_two, a_in[:, 4:], preferred_element_type=WIDE)
        * adapter_picks[:, None, :]
    ).astype(NARROW)
    gate_up = jnp.einsum(
        "td,djf->tjf", xn_two, w_gate_up, preferred_element_type=WIDE
    ) + jnp.einsum("tjr,jrf->tjf", u_two, b_ffn, preferred_element_type=WIDE)
    hidden = (jax.nn.silu(gate_up[:, 0]) * gate_up[:, 1]).astype(NARROW)
    u_down = fast_dot(hidden, a_down) * adapter_picks
    return {
        "scale_one": scale_one,
        "xn_one": xn_one,
        "u_one": u_one,
        "strength": strength,
        "core_back": core_back,
        "carried": carried_state_rows,
        "trans_map": trans_map,
        "state_in": incoming_state_value,
        "mixer_out": mixer_output_rows,
        "mixer_scale": mixer_scale,
        "normed": normed,
        "u_out": u_out,
        "hidden_one": hidden_one,
        "scale_two": scale_two,
        "xn_two": xn_two,
        "u_two": u_two,
        "gate_up": gate_up,
        "hidden": hidden,
        "u_down": u_down,
    }


def on_device(
    layer_in,
    cotangent,
    segments,
    adapters,
    norm_one,
    norm_two,
    out_gain,
    beta_bias,
    conv_taps,
    w_qkv,
    w_beta,
    w_out,
    w_gate_up,
    w_down,
    a_in,
    b_heads,
    b_beta,
    a_out,
    b_ffn,
    a_down,
    b_res,
):
    shards = (
        w_qkv,
        w_beta,
        w_out,
        w_gate_up,
        w_down,
        a_in,
        b_heads,
        b_beta,
        a_out,
        b_ffn,
        a_down,
        b_res,
    )
    row_count = layer_in.shape[0]
    seg_count = adapters.shape[0]
    rank_total = a_in.shape[2]
    per_token = jnp.sum(
        jnp.where(
            segments[:, None] == jnp.arange(seg_count, dtype=jnp.int32)[None, :],
            adapters[None, :],
            0,
        ),
        axis=1,
    )
    owner_ids = jnp.arange(rank_total, dtype=jnp.int32) // RANK
    adapter_picks = (per_token[:, None] == owner_ids[None, :]).astype(WIDE)
    weights = fetch_weights(*shards)
    forward_values = forward_pass(
        layer_in,
        segments,
        adapter_picks,
        norm_one,
        norm_two,
        out_gain,
        beta_bias,
        conv_taps,
        weights,
    )
    partial_ffn = fast_dot(forward_values["hidden"], weights[7]) + precise_dot(
        forward_values["u_down"], weights[11][1].astype(WIDE)
    )
    ffn_share = lax.psum_scatter(
        partial_ffn.astype(jnp.bfloat16), "mp", scatter_dimension=1, tiled=True
    ).astype(jnp.float32)
    share_width = ffn_share.shape[1]
    start_col = lax.axis_index("mp") * share_width
    output = (
        lax.dynamic_slice_in_dim(forward_values["hidden_one"], start_col, share_width, 1)
        + ffn_share
    ).astype(NARROW)
    grad_out_full = lax.all_gather(cotangent, "mp", axis=1, tiled=True)
    barriered = lax.optimization_barrier((grad_out_full, layer_in) + shards)
    grad_out_full = barriered[0]
    input_back = barriered[1]
    weights_back = fetch_weights(*barriered[2:])
    stored_value_rows = forward_pass(
        input_back,
        segments,
        adapter_picks,
        norm_one,
        norm_two,
        out_gain,
        beta_bias,
        conv_taps,
        weights_back,
    )
    (
        w_qkv_b,
        w_beta_b,
        w_out_b,
        b_heads_b,
        b_beta_b,
        a_out_b,
        w_gate_up_b,
        w_down_b,
        b_ffn_b,
        a_down_b,
        a_in_b,
        b_res_b,
    ) = weights_back
    grad_wide = grad_out_full.astype(WIDE)
    hidden = stored_value_rows["hidden"]
    e_down = fast_dot(grad_out_full, b_res_b[1].T) * adapter_picks
    grad_b_res_down = precise_dot(stored_value_rows["u_down"].T, grad_wide)
    grad_a_down = precise_dot(hidden.astype(WIDE).T, e_down)
    d_hidden = fast_dot(grad_out_full, w_down_b.T) + precise_dot(e_down, a_down_b.astype(WIDE).T)
    gate_pre = stored_value_rows["gate_up"][:, 0]
    up_part = stored_value_rows["gate_up"][:, 1]
    sig_gate = jax.nn.sigmoid(gate_pre)
    d_gate = d_hidden * up_part * sig_gate * (1.0 + gate_pre * (1.0 - sig_gate))
    d_up = d_hidden * gate_pre * sig_gate
    d_gate_up = jnp.stack([d_gate, d_up], axis=1).astype(NARROW)
    e_two = (
        jnp.einsum("tjf,jrf->tjr", d_gate_up, b_ffn_b, preferred_element_type=WIDE)
        * adapter_picks[:, None, :]
    )
    grad_b_ffn = jnp.einsum(
        "tjr,tjf->jrf", stored_value_rows["u_two"], d_gate_up, preferred_element_type=WIDE
    )
    grad_a_in_ffn = jnp.einsum(
        "td,tjr->djr", stored_value_rows["xn_two"].astype(WIDE), e_two, precision=EXACT_PRECISION
    )
    d_xn_two_part = jnp.einsum(
        "tjf,djf->td", d_gate_up, w_gate_up_b, preferred_element_type=WIDE
    ) + jnp.einsum("tjr,djr->td", e_two, a_in_b[:, 4:].astype(WIDE), precision=EXACT_PRECISION)
    d_xn_two = lax.psum(d_xn_two_part.astype(jnp.bfloat16), "mp").astype(jnp.float32)
    d_hidden_one = grad_wide + norm_back(
        stored_value_rows["hidden_one"], stored_value_rows["scale_two"], norm_two, d_xn_two
    )
    d_branch = d_hidden_one.astype(NARROW)
    e_out = fast_dot(d_branch, b_res_b[0].T) * adapter_picks
    grad_b_res_mix = precise_dot(stored_value_rows["u_out"].T, d_branch.astype(WIDE))
    grad_a_out = precise_dot(stored_value_rows["normed"].astype(WIDE).T, e_out)
    d_normed = fast_dot(d_branch, w_out_b.T) + precise_dot(e_out, a_out_b.astype(WIDE).T)
    mixer_output_rows = stored_value_rows["mixer_out"]
    mixer_output_gradient = norm_back(
        mixer_output_rows,
        stored_value_rows["mixer_scale"],
        out_gain,
        d_normed.reshape(mixer_output_rows.shape),
    )
    incoming_state_value = stored_value_rows["state_in"]
    segment_local_gradient = jnp.einsum(
        "oie,oil->iel",
        stored_value_rows["carried"],
        mixer_output_gradient,
        precision=EXACT_PRECISION,
    )
    carried_state_gradient = jnp.einsum(
        "dlu,lbu->dlb", mixer_output_gradient, incoming_state_value, precision=EXACT_PRECISION
    )
    trans_t = jnp.swapaxes(stored_value_rows["trans_map"], 1, 2)
    identity_maps = jnp.broadcast_to(jnp.eye(DH, dtype=WIDE), trans_t.shape)
    outgoing = prefix(
        (trans_t, segment_local_gradient),
        "dp",
        compose,
        (identity_maps, jnp.zeros_like(segment_local_gradient)),
    )
    final_state_gradient = outgoing[1]
    transition_gradient = jnp.einsum(
        "gnw,gow->gno", final_state_gradient, incoming_state_value, precision=EXACT_PRECISION
    )
    d_pre_ext, d_strength = stored_value_rows["core_back"](
        (mixer_output_gradient, carried_state_gradient, transition_gradient, final_state_gradient)
    )
    from_next = from_behind(d_pre_ext[: KW - 1], "dp", -1)
    d_pre_wide = d_pre_ext[KW - 1 :].at[row_count - KW + 1 :].add(from_next)
    d_pre = d_pre_wide.astype(NARROW)
    strength = stored_value_rows["strength"]
    d_logit = d_strength * strength * (1.0 - strength)
    e_heads = jnp.einsum("tjc,jrc->tjr", d_pre, b_heads_b, preferred_element_type=WIDE)
    e_beta = precise_dot(d_logit, b_beta_b.astype(WIDE).T)
    e_one = jnp.concatenate([e_heads, e_beta[:, None, :]], axis=1) * adapter_picks[:, None, :]
    u_one = stored_value_rows["u_one"]
    grad_b_heads = jnp.einsum("tjr,tjc->jrc", u_one[:, :3], d_pre, preferred_element_type=WIDE)
    grad_b_beta = precise_dot(u_one[:, 3].astype(WIDE).T, d_logit)
    grad_a_in_mix = jnp.einsum(
        "td,tjr->djr", stored_value_rows["xn_one"].astype(WIDE), e_one, precision=EXACT_PRECISION
    )
    d_xn_one_part = (
        jnp.einsum("tjc,djc->td", d_pre, w_qkv_b, preferred_element_type=WIDE)
        + precise_dot(d_logit, w_beta_b.astype(WIDE).T)
        + jnp.einsum("tjr,djr->td", e_one, a_in_b[:, :4].astype(WIDE), precision=EXACT_PRECISION)
    )
    d_xn_one = lax.psum(d_xn_one_part.astype(jnp.bfloat16), "mp").astype(jnp.float32)
    grad_full = d_hidden_one + norm_back(
        input_back.astype(WIDE), stored_value_rows["scale_one"], norm_one, d_xn_one
    )
    grad_input = lax.dynamic_slice_in_dim(grad_full, start_col, share_width, 1)
    factor_parts = (
        lax.psum_scatter(
            grad_b_heads.astype(jnp.bfloat16), "dp", scatter_dimension=1, tiled=True
        ).astype(jnp.float32),
        lax.psum_scatter(
            grad_b_beta.astype(jnp.bfloat16), "dp", scatter_dimension=0, tiled=True
        ).astype(jnp.float32),
        lax.psum_scatter(
            grad_a_out.astype(jnp.bfloat16), "dp", scatter_dimension=1, tiled=True
        ).astype(jnp.float32),
        lax.psum_scatter(
            grad_b_ffn.astype(jnp.bfloat16), "dp", scatter_dimension=1, tiled=True
        ).astype(jnp.float32),
        lax.psum_scatter(
            grad_a_down.astype(jnp.bfloat16), "dp", scatter_dimension=1, tiled=True
        ).astype(jnp.float32),
    )
    shared_parts = (
        lax.psum_scatter(
            jnp.concatenate([grad_a_in_mix, grad_a_in_ffn], axis=1),
            ("dp", "mp"),
            scatter_dimension=0,
            tiled=True,
        ),
        lax.psum_scatter(
            jnp.stack([grad_b_res_mix, grad_b_res_down]),
            ("dp", "mp"),
            scatter_dimension=2,
            tiled=True,
        ),
    )
    return (
        output,
        grad_input,
        shared_parts[0],
        factor_parts[0],
        factor_parts[1],
        factor_parts[2],
        factor_parts[3],
        factor_parts[4],
        shared_parts[1],
    )


def solution(mesh):
    placed = (
        P("dp", None),
        P("dp", "mp"),
        P("dp"),
        P(),
        P(),
        P(),
        P(),
        P("mp"),
        P(None, None, "mp"),
        P("dp", None, "mp"),
        P("dp", "mp"),
        P("mp", "dp"),
        P("dp", None, "mp"),
        P("mp", "dp"),
        P(("dp", "mp"), None, None),
        P(None, "dp", "mp"),
        P("dp", "mp"),
        P("mp", "dp"),
        P(None, "dp", "mp"),
        P("mp", "dp"),
        P(None, None, ("dp", "mp")),
    )
    return jax.shard_map(
        on_device,
        mesh=mesh,
        in_specs=placed,
        out_specs=(
            P("dp", "mp"),
            P("dp", "mp"),
            P(("dp", "mp"), None, None),
            P(None, "dp", "mp"),
            P("dp", "mp"),
            P("mp", "dp"),
            P(None, "dp", "mp"),
            P("mp", "dp"),
            P(None, None, ("dp", "mp")),
        ),
        check_vma=False,
    )
```

profile of v0, /device:TPU:1, one launch (start us, length us, event | category | flops | bytes accessed | tf_op | source)
XLA Modules:
  0.0 2151.8 jit_solution(4171631136737270947)
XLA Ops:
  8.7 27.2 %all-gather.46.cloned.1.call-done = bf16[256,2048]{1,0:T(8,128)(2,1)} async-done(((bf16[256,512]{1,0:T(8,128)(2,1)}), bf16[256,2048]{1,0:T(8,128)(2,1)}) %all-gather.46.cloned.1.call-update) | async-done | bytes 1048592 | tf_op jit(solution)/shard_map/all_gather | solution.py:360
  143.3 32.7 %all-gather.50.cloned.1.call-done = bf16[2048,6,128]{2,0,1:T(8,128)(2,1)} async-done(((bf16[16,6,128]{2,0,1:T(8,128)(2,1)}), bf16[2048,6,128]{2,0,1:T(8,128)(2,1)}) %all-gather.50.cloned.1.call-update) | async-done | bytes 3145744 | tf_op jit(solution)/shard_map/all_gather | solution.py:199
  179.1 47.4 %all-gather.34.cloned.1.call-done = bf16[2048,3,512]{2,0,1:T(8,128)(2,1)} async-done(((bf16[64,3,512]{2,0,1:T(8,128)(2,1)}), bf16[2048,3,512]{2,0,1:T(8,128)(2,1)}) %all-gather.34.cloned.1.call-update) | async-done | bytes 6291472 | tf_op jit(solution)/shard_map/all_gather | solution.py:185
  234.2 42.6 %all-gather.48.cloned.1.call-done = bf16[2048,3,512]{2,0,1:T(8,128)(2,1)} async-done(((bf16[64,3,512]{2,0,1:T(8,128)(2,1)}), bf16[2048,3,512]{2,0,1:T(8,128)(2,1)}) %all-gather.48.cloned.1.call-update) | async-done | bytes 6291472 | tf_op jit(solution)/shard_map/all_gather | solution.py:185
  301.9 120.3 %while.152 = (s32[]{:T(128)}, f32[4,128,128]{2,1,0:T(8,128)S(1)}, f32[4,128,128]{2,1,0:T(8,128)S(1)}, f32[4,4,64,128]{3,2,0,1:T(8,128)}, f32[4,4,64,128]{3,2,0,1...) while((s32[]{:T(128)}, f32[4,128,128]{2,1,0:T(8,128)S(1)}, ...), condition=%wide.region_5.7_spmd.clone, body=%wide.region_4.6_spmd.clone.sunk | while | flops 504246528 | bytes 7581988 | solution.py:175
  423.3 26.9 %all-gather.10 = bf16[32,64,4]{1,2,0:T(4,128)(2,1)S(1)} all-gather(bf16[1,64,4]{1,2,0:T(4,128)(2,1)S(1)} %bitcast.923), channel_id=1, replica_groups=mesh['dp'=32,'mp'=4] {'dp'}, dimensions={0}, use_global_device_ids=true | all-gather | bytes 16896 | tf_op jit(solution)/shard_map/all_gather | solution.py:186
  485.3 159.0 %while.156 = (s32[]{:T(128)}, f32[4,128,128]{2,1,0:T(8,128)S(1)}, f32[4,128,128]{2,1,0:T(8,128)S(1)}, f32[4,4,64,128]{3,2,0,1:T(8,128)}, f32[4,4,64,128]{3,2,0,1...) while((s32[]{:T(128)}, f32[4,128,128]{2,1,0:T(8,128)S(1)}, ...), condition=%wide.region_16.18_spmd.clone.clone, body=%wide.region_15.17_spmd.clone.clone.sunk | while | flops 504488384 | bytes 11570489 | solution.py:175
  698.2 46.1 %while.153 = (s32[]{:T(128)}, f32[4,128,128]{2,1,0:T(8,128)S(1)}, s32[]{:T(128)}, f32[32,4,128,128]{3,2,1,0:T(8,128)}, f32[32,4,128,128]{3,2,1,0:T(8,128)}, /*index=5*/s32[]{:T(128)}, s32[]{:T(128)}) while((s32[]{:T(128)}, f32[4,128,128]{2,1,0:T(8,128)S(1)}, s32[]{:T(128)}, f32[32,4,128,128]{3,2,1,0:T(8,128)}, ...), condition=%wide.region_7.9_spmd.clone, body=%wide.region_6.8_spmd.clone.sunk | while | flops 100925440 | bytes 1837671 | solution.py:35
  752.9 46.0 %while.154 = (s32[]{:T(128)}, f32[4,128,128]{2,1,0:T(8,128)S(1)}, s32[]{:T(128)}, f32[32,4,128,128]{3,2,1,0:T(8,128)}, f32[32,4,128,128]{3,2,1,0:T(8,128)}, /*index=5*/s32[]{:T(128)}, s32[]{:T(128)}) while((s32[]{:T(128)}, f32[4,128,128]{2,1,0:T(8,128)S(1)}, s32[]{:T(128)}, f32[32,4,128,128]{3,2,1,0:T(8,128)}, ...), condition=%wide.region_18.20_spmd.clone, body=%wide.region_17.19_spmd.clone.sunk | while | flops 100925440 | bytes 1837671 | solution.py:35
  820.7 62.1 %all-gather.54.cloned.1.call-done = bf16[2,128,2048]{1,2,0:T(8,128)(2,1)} async-done(((bf16[2,128,16]{1,2,0:T(8,128)(2,1)}), bf16[2,128,2048]{1,2,0:T(8,128)(2,1)}) %all-gather.54.cloned.1.call-update) | async-done | bytes 1048592 | tf_op jit(solution)/shard_map/all_gather | solution.py:200
  886.2 40.6 %all-gather.38.cloned.1.call-done = bf16[512,2048]{0,1:T(8,128)(2,1)} async-done(((bf16[512,64]{0,1:T(8,128)(2,1)}), bf16[512,2048]{0,1:T(8,128)(2,1)}) %all-gather.38.cloned.1.call-update) | async-done | bytes 2097168 | tf_op jit(solution)/shard_map/all_gather | solution.py:187
  930.5 41.8 %all-gather.52.cloned.1.call-done = bf16[512,2048]{0,1:T(8,128)(2,1)} async-done(((bf16[512,64]{0,1:T(8,128)(2,1)}), bf16[512,2048]{0,1:T(8,128)(2,1)}) %all-gather.52.cloned.1.call-update) | async-done | bytes 2097168 | tf_op jit(solution)/shard_map/all_gather | solution.py:187
  1003.6 25.7 %all_gather.143 = bf16[2,128,1408]{2,0,1:T(2,128)(2,1)} all-gather(bf16[2,4,1408]{2,0,1:T(2,128)(2,1)S(1)} %copy.483), channel_id=1, replica_groups=mesh['dp'=32,'mp'=4] {'dp'}, dimensions={1}, use_global_device_ids=true | all-gather | bytes 743424 | tf_op jit(solution)/shard_map/all_gather | solution.py:195
  1037.2 79.2 %all-reduce.29.cloned.1.call-done = (f32[256,2048]{1,0:T(8,128)}, f32[256,2048]{1,0:T(8,128)}) async-done(((f32[256,2048]{1,0:T(8,128)}, f32[256,2048]{1,0:T(8,128)}), (f32[256,2048]{1,0:T(8,128)}, f32[256,2048]{1,0:T(8,128)})) %all-reduce.29.cloned.1.call-update) | async-done | bytes 4194320 | tf_op jit(solution)/shard_map/psum | solution.py:250
  1121.7 58.0 %all-gather.58.cloned.1.call-done = bf16[2048,2,1408]{2,0,1:T(8,128)(2,1)} async-done(((bf16[64,2,1408]{2,0,1:T(8,128)(2,1)}), bf16[2048,2,1408]{2,0,1:T(8,128)(2,1)}) %all-gather.58.cloned.1.call-update) | async-done | bytes 11534352 | tf_op jit(solution)/shard_map/all_gather | solution.py:193
  1203.8 39.9 %all-reduce.23.cloned.1.call-done = bf16[256,2048]{1,0:T(8,128)(2,1)} async-done(((bf16[256,2048]{1,0:T(8,128)(2,1)}), bf16[256,2048]{1,0:T(8,128)(2,1)}) %all-reduce.23.cloned.1.call-update) | async-done | bytes 1048592 | tf_op jit(solution)/shard_map/psum | solution.py:415
  1259.5 29.8 %all-gather.9 = bf16[32,4,1408]{2,1,0:T(4,128)(2,1)} all-gather(bf16[1,4,1408]{2,1,0:T(4,128)(2,1)} %bitcast.918), channel_id=1, replica_groups=mesh['dp'=32,'mp'=4] {'dp'}, dimensions={0}, use_global_device_ids=true | all-gather | bytes 371712 | tf_op jit(solution)/shard_map/all_gather | solution.py:196
  1291.1 25.9 %all_gather.124 = bf16[2,128,1408]{2,0,1:T(2,128)(2,1)} all-gather(bf16[2,4,1408]{2,0,1:T(2,128)(2,1)} %copy.465), channel_id=1, replica_groups=mesh['dp'=32,'mp'=4] {'dp'}, dimensions={1}, use_global_device_ids=true | all-gather | bytes 743424 | tf_op jit(solution)/shard_map/all_gather | solution.py:195
  1373.5 34.5 %all-gather.70.cloned.1.call-done = bf16[128,128,128]{2,1,0:T(8,128)(2,1)} async-done(((bf16[4,128,128]{2,1,0:T(8,128)(2,1)}), bf16[128,128,128]{2,1,0:T(8,128)(2,1)}) %all-gather.70.cloned.1.call-update) | async-done | bytes 4194320 | tf_op jit(solution)/shard_map/all_gather | solution.py:41
  1408.0 48.0 %all-gather.68.cloned.1.call-done = bf16[128,128,128]{2,1,0:T(8,128)(2,1)} async-done(((bf16[4,128,128]{2,1,0:T(8,128)(2,1)}), bf16[128,128,128]{2,1,0:T(8,128)(2,1)}) %all-gather.68.cloned.1.call-update) | async-done | bytes 4194320 | tf_op jit(solution)/shard_map/all_gather | solution.py:41
  1456.0 42.4 %while.155 = (s32[]{:T(128)}, f32[4,128,128]{2,1,0:T(8,128)S(1)}, s32[]{:T(128)}, bf16[32,4,128,128]{3,2,1,0:T(8,128)(2,1)}, bf16[32,4,128,128]{3,2,1,0:T(8,128)...) while((s32[]{:T(128)}, f32[4,128,128]{2,1,0:T(8,128)S(1)}, s32[]{:T(128)}, ...), condition=%wide.region_26.28_spmd.clone, body=%wide.region_25.27_spmd.clone.sunk | while | flops 100990984 | bytes 1575589 | solution.py:59
  1502.3 243.8 %while.151 = (s32[]{:T(128)}, f32[4,128,128]{2,1,0:T(8,128)S(1)}, f32[4,128,128]{2,1,0:T(8,128)S(1)}, f32[4,64,4,128]{3,1,2,0:T(8,128)}, f32[4,64,4,128]{3,1,2,0...) while((s32[]{:T(128)}, f32[4,128,128]{2,1,0:T(8,128)S(1)}, ...), condition=%wide.region_30.32_spmd.clone, body=%wide.region_27.31_spmd.clone.sunk | while | flops 1020636992 | bytes 16780312 | solution.py:175
  1798.1 121.0 %all-reduce.10 = bf16[128,4]{1,0:T(8,128)(2,1)S(1)} all-reduce(bf16[128,4]{1,0:T(8,128)(2,1)S(1)} %convolution_convert_fusion.5), channel_id=11, replica_groups=mesh['dp'=32,'mp'=4] {'dp'}, use_global_device_ids=true, to_apply=%region_37.39.clone | all-reduce | flops 512 | bytes 2048
  1930.3 214.7 %reduce-scatter.7.cloned.1.call-done = f32[16,6,128]{2,0,1:T(8,128)} async-done(((f32[2048,6,128]{2,0,1:T(8,128)}), f32[16,6,128]{2,0,1:T(8,128)}) %reduce-scatter.7.cloned.1.call-update) | async-done | bytes 49168 | tf_op jit(solution)/shard_map/reduce_scatter | solution.py:498
  (1184 shorter events, 1131.0 us)
Async XLA Ops:
  7.9 132.7 %all-gather.36.cloned.1.call-start = ((), (), s32[]{:S(2)}) async-start(), calls=%async_computation.3 | async-start | bytes 3170304 | tf_op jit(solution)/shard_map/all_gather | solution.py:199
  8.7 167.3 %all-gather.50.cloned.1.call-start = ((), (), s32[]{:S(2)}) async-start(), calls=%async_computation.11 | async-start | bytes 3170304 | tf_op jit(solution)/shard_map/all_gather | solution.py:199
  36.0 190.5 %all-gather.34.cloned.1.call-start = ((), (), s32[]{:S(2)}) async-start(), calls=%async_computation.2 | async-start | bytes 6488064 | tf_op jit(solution)/shard_map/all_gather | solution.py:185
  36.6 240.3 %all-gather.48.cloned.1.call-start = ((), (), s32[]{:S(2)}) async-start(), calls=%async_computation.10 | async-start | bytes 6488064 | tf_op jit(solution)/shard_map/all_gather | solution.py:185
  37.2 661.0 %all-gather.60.cloned.1.call-start = ((), (), s32[]{:S(2)}) async-start(), calls=%async_computation.19 | async-start | bytes 8650752 | tf_op jit(solution)/shard_map/all_gather | solution.py:26
  423.0 275.2 %all-gather.62.cloned.1.call-start = ((), (), s32[]{:S(2)}) async-start(), calls=%async_computation.20 | async-start | bytes 8650752 | tf_op jit(solution)/shard_map/all_gather | solution.py:26
  483.1 263.1 %all-gather.64.cloned.1.call-start = ((), (), s32[]{:S(2)}) async-start(), calls=%async_computation.21 | async-start | bytes 8650752 | tf_op jit(solution)/shard_map/all_gather | solution.py:26
  645.8 172.8 %all-gather.40.cloned.1.call-start = ((), (), s32[]{:S(2)}) async-start(), calls=%async_computation.5 | async-start | bytes 1056768 | tf_op jit(solution)/shard_map/all_gather | solution.py:200
  646.4 236.4 %all-gather.54.cloned.1.call-start = ((), (), s32[]{:S(2)}) async-start(), calls=%async_computation.13 | async-start | bytes 1056768 | tf_op jit(solution)/shard_map/all_gather | solution.py:200
  647.1 279.6 %all-gather.38.cloned.1.call-start = ((), (), s32[]{:S(2)}) async-start(), calls=%async_computation.4 | async-start | bytes 2162688 | tf_op jit(solution)/shard_map/all_gather | solution.py:187
  647.7 324.6 %all-gather.52.cloned.1.call-start = ((), (), s32[]{:S(2)}) async-start(), calls=%async_computation.12 | async-start | bytes 2162688 | tf_op jit(solution)/shard_map/all_gather | solution.py:187
  648.4 382.5 %all-gather.56.cloned.1.call-start = ((), (), s32[]{:S(2)}) async-start(), calls=%async_computation.14 | async-start | bytes 5947392 | tf_op jit(solution)/shard_map/all_gather | solution.py:194
  695.7 420.8 %all-reduce.29.cloned.1.call-start = ((), (), s32[]{:S(2)}) async-start(), calls=%async_computation.26 | async-start | bytes 8388608 | tf_op jit(solution)/shard_map/psum | solution.py:250
  976.6 203.1 %all-gather.58.cloned.1.call-start = ((), (), s32[]{:S(2)}) async-start(), calls=%async_computation.15 | async-start | bytes 11894784 | tf_op jit(solution)/shard_map/all_gather | solution.py:193
  978.4 265.3 %all-reduce.23.cloned.1.call-start = ((), (), s32[]{:S(2)}) async-start(), calls=%async_computation.16 | async-start | bytes 2097152 | tf_op jit(solution)/shard_map/psum | solution.py:415
  1200.1 136.8 %all-gather.42.cloned.1.call-start = ((), (), s32[]{:S(2)}) async-start(), calls=%async_computation.6 | async-start | bytes 11894784 | tf_op jit(solution)/shard_map/all_gather | solution.py:193
  1202.0 161.6 %all-gather.44.cloned.1.call-start = ((), (), s32[]{:S(2)}) async-start(), calls=%async_computation.7 | async-start | bytes 5947392 | tf_op jit(solution)/shard_map/all_gather | solution.py:194
  1202.7 205.3 %all-gather.70.cloned.1.call-start = ((), (), s32[]{:S(2)}) async-start(), calls=%async_computation.24 | async-start | bytes 4325376 | tf_op jit(solution)/shard_map/all_gather | solution.py:41
  1203.5 252.5 %all-gather.68.cloned.1.call-start = ((), (), s32[]{:S(2)}) async-start(), calls=%async_computation.23 | async-start | bytes 4325376 | tf_op jit(solution)/shard_map/all_gather | solution.py:41
  1258.8 535.0 %all-reduce.27.cloned.1.call-start = ((), (), s32[]{:S(2)}) async-start(), calls=%async_computation.25 | async-start | bytes 4194304
  1360.0 435.1 %reduce-scatter.5.cloned.1.call-start = ((), (), s32[]{:S(2)}) async-start(), calls=%async_computation.8 | async-start | bytes 1310720 | tf_op jit(solution)/shard_map/reduce_scatter | solution.py:351
  1370.2 549.4 %all-reduce.31.cloned.1.call-start = ((), (), s32[]{:S(2)}) async-start(), calls=%async_computation.27 | async-start | bytes 3211264
  1774.5 152.1 %all-reduce.25.cloned.1.call-start = ((), (), s32[]{:S(2)}) async-start(), calls=%async_computation.17 | async-start | bytes 2097152 | tf_op jit(solution)/shard_map/psum | solution.py:475
  1784.0 361.0 %reduce-scatter.7.cloned.1.call-start = ((), (), s32[]{:S(2)}) async-start(), calls=%async_computation.18 | async-start | bytes 6340608 | tf_op jit(solution)/shard_map/reduce_scatter | solution.py:498
  (149 other events, 5779.4 us)
Sparse Core Ops, SparseCore 0:
  38.8 68.3 all-gather.35
  110.1 65.8 all-gather.49
  178.2 48.2 all-gather.33
  228.7 48.1 all-gather.47
  423.1 54.5 all-gather.59
  483.2 52.9 all-gather.61
  645.2 52.7 all-gather.63
  700.3 52.5 all-gather.65
  755.6 63.0 all-gather.39
  821.5 61.2 all-gather.53
  884.9 41.7 all-gather.37
  929.0 43.2 all-gather.51
  974.4 48.3 all-gather.55
  1025.1 91.3 all-reduce.28
  1118.9 60.8 all-gather.57
  1200.3 43.3 all-reduce.22
  1245.8 64.4 all-gather.41
  1312.5 47.8 all-gather.43
  1362.5 45.4 all-gather.69
  1410.3 45.6 all-gather.67
  1460.8 149.8 all-reduce.26
  1774.6 105.5 all-reduce.30
  1882.7 43.9 all-reduce.24
  1932.0 213.0 reduce-scatter.6
  (2 shorter events, 46.3 us)
where the time goes:
time: 2170 us; the launch traced here: 2150 us
  waiting for transfers between devices  800 us (37%)
  matrix products  443 us (20%)
  blocking collectives  415 us (19%)
  other arithmetic  320 us (15%)
  local copies, waits for them, and re-layouts  136 us (6%)
    another operation x44, other arithmetic, piece_step(): lax.linalg.triangular_solve(lower_part, right_side, left_side=True, lower...  241 us
    reduce_scatter x1, waiting for transfers between devices, on_device(): lax.psum_scatter(jnp.concatenate([grad_a_in_mix, grad_a_in_ffn], axis=1),...  215 us
    dot_general x94, matrix products, compose(): jnp.einsum('hij,hjk->hik', later[0], earlier[1], precision=EXACT_PRECISION)  129 us
    unnamed x1, blocking collectives  121 us
    all_gather x2, waiting for transfers between devices, fetch_weights(): lax.all_gather(w_qkv, 'dp', axis=0, tiled=True)  90.1 us
    all_gather x2, waiting for transfers between devices, prefix(): lax.all_gather(part.astype(kind), axis)  82.5 us
    all_gather x2, waiting for transfers between devices, fetch_weights(): lax.all_gather(w_out, 'dp', axis=1, tiled=True)  82.3 us
    psum x1, waiting for transfers between devices, forward_pass(): branch = lax.psum(partial_mix, 'mp')  79.2 us
  transfers between devices with their start and end apart: 30, of which 17 were waited for; matrix products, arithmetic and copies ran while one was open for 34% of the time, Pallas kernels for 0%

commit v1 on v0

v1 whole, which is shorter than its diff:
```python
import functools

import jax
import jax.numpy as jnp
from jax import lax
from jax.experimental import pallas as pl
from jax.experimental.pallas import tpu as pltpu
from jax.sharding import PartitionSpec as P

DH = 128
KW = 4
RANK = 16
HALO = 16
EPSILON = 1e-06
WIDE = jnp.float32
NARROW = jnp.bfloat16
MESH = pl.DeviceIdType.MESH
EXACT = lax.Precision.HIGHEST


def coords():
    place = lax.axis_index("dp")
    return place // 8, lax.rem(place // 2, 4), lax.rem(place, 2)


def place_of(y, z, c):
    return (y * 4 + z) * 2 + c


def moved(dy, dz, other_core=False):
    y, z, c = coords()
    return place_of(lax.rem(y + dy + 4, 4), lax.rem(z + dz + 4, 4), 1 - c if other_core else c)


def greet(dp_peers=(), mp_peers=()):
    barrier = pltpu.get_barrier_semaphore()
    for peer in dp_peers:
        pl.semaphore_signal(barrier, inc=1, device_id={"dp": peer}, device_id_type=MESH)
    for peer in mp_peers:
        pl.semaphore_signal(barrier, inc=1, device_id={"mp": peer}, device_id_type=MESH)
    pl.semaphore_wait(barrier, len(dp_peers) + len(mp_peers))


class Mailbox:
    def __init__(self, send, recv):
        self.send, self.recv, self.copies = send, recv, []

    def push(self, src, dst, **device):
        k = len(self.copies)
        copy = pltpu.make_async_remote_copy(
            src_ref=src,
            dst_ref=dst,
            send_sem=self.send.at[k],
            recv_sem=self.recv.at[k],
            device_id=device,
            device_id_type=MESH,
        )
        copy.start()
        self.copies.append(copy)
        return copy

    def drain(self):
        for copy in self.copies:
            copy.wait_send()


def gather_steps(box, own, out):
    me = moved(0, 0)
    half = own.shape[0] // 2
    quarter = half // 2
    sibling = moved(0, 0, True)
    kinds = []
    for kind in range(2):
        base = kind * half
        parts = (pl.ds(base, half), pl.ds(base, quarter), pl.ds(base + quarter, quarter))
        if kind == 0:
            kinds.append((parts, lambda a, b: moved(a, b)))
        else:
            kinds.append((parts, lambda a, b: moved(b, a)))
    near, across, far, far_across, shared = [], [{}, {}], [[], []], [{}, {}], []

    def open_up():
        for parts, at in kinds:
            near.append([box.push(own.at[parts[0]], out.at[me, parts[0]], dp=at(s, 0)) for s in (1, -1)])
        for k, (parts, at) in enumerate(kinds):
            across[k][0] = [box.push(own.at[parts[0]], out.at[me, parts[0]], dp=at(0, s)) for s in (1, -1)]
        shared.append(box.push(own, out.at[me], dp=sibling))

    def pass_on(k, slot):
        parts, at = kinds[k]
        block = out.at[slot, parts[0]]
        return [box.push(block, block, dp=at(0, t)) for t in (1, -1)]

    def to_sibling(k, slot):
        block = out.at[slot, kinds[k][0][0]]
        shared.append(box.push(block, block, dp=sibling))

    def from_near(i, s):
        def step():
            for k, (parts, at) in enumerate(kinds):
                near[k][i].wait_recv()
                block = out.at[at(s, 0), parts[1 + i]]
                far[k].append(box.push(block, block, dp=at(-s, 0)))
            for k, (parts, at) in enumerate(kinds):
                across[k][s] = pass_on(k, at(s, 0))
                to_sibling(k, at(s, 0))

        return step

    def from_far(k):
        def step():
            for copy in far[k]:
                copy.wait_recv()
            slot = kinds[k][1](2, 0)
            across[k][2] = pass_on(k, slot)
            to_sibling(k, slot)

        return step

    def from_across(k, f):
        def step():
            parts, at = kinds[k]
            far_across[k][f] = []
            for i, s in enumerate((-1, 1)):
                across[k][f][i].wait_recv()
                slot = at(f, s)
                block = out.at[slot, parts[1 + i]]
                far_across[k][f].append(box.push(block, block, dp=at(0, -s)))
                to_sibling(k, slot)

        return step

    def from_far_across(k, f):
        def step():
            for copy in far_across[k][f]:
                copy.wait_recv()
            to_sibling(k, kinds[k][1](f, 2))

        return step

    def close():
        for copy in shared:
            copy.wait_recv()

    steps = [open_up, from_near(0, -1), from_near(1, 1), from_far(0), from_far(1)]
    steps += [from_across(k, f) for f in (0, -1, 1, 2) for k in range(2)]
    steps += [from_far_across(k, f) for f in (0, -1, 1, 2) for k in range(2)]
    return steps + [close]


def gather_peers():
    return [moved(1, 0), moved(-1, 0), moved(0, 1), moved(0, -1), moved(0, 0, True)]


GATHER_COPIES = 71


def first_gather_kernel(wide_ref, thin_ref, wide_out, thin_out, thin_own, send, recv, local):
    m = lax.axis_index("mp")
    mp_peers = [lax.rem(m + k, 4) for k in (1, 2, 3)]
    greet(gather_peers(), mp_peers)
    me = moved(0, 0)
    box = Mailbox(send, recv)
    rows = thin_ref.shape[0]
    mine = pl.ds(pl.multiple_of(m * rows, rows), rows)
    crossing = [box.push(thin_ref, thin_own.at[mine], mp=peer) for peer in mp_peers]
    keep_wide = pltpu.make_async_copy(wide_ref, wide_out.at[me], local.at[0])
    keep_wide.start()
    keep_thin = pltpu.make_async_copy(thin_ref, thin_own.at[mine], local.at[1])
    keep_thin.start()
    wide_steps = gather_steps(box, wide_ref, wide_out)
    thin_steps = gather_steps(box, thin_own, thin_out)
    wide_steps[0]()
    keep_thin.wait()
    for copy in crossing:
        copy.wait_recv()
    keep_thin_out = pltpu.make_async_copy(thin_own, thin_out.at[me], local.at[2])
    keep_thin_out.start()
    thin_steps[0]()
    for one, two in zip(wide_steps[1:], thin_steps[1:]):
        one()
        two()
    keep_wide.wait()
    keep_thin_out.wait()
    box.drain()


def first_gather(wide, thin):
    count = 2 * GATHER_COPIES + 3
    rows, cols = thin.shape
    anywhere = pl.BlockSpec(memory_space=pl.ANY)
    return pl.pallas_call(
        first_gather_kernel,
        out_shape=(
            jax.ShapeDtypeStruct((32,) + wide.shape, wide.dtype),
            jax.ShapeDtypeStruct((32, 4 * rows, cols), thin.dtype),
        ),
        in_specs=[anywhere, anywhere],
        out_specs=(anywhere, anywhere),
        scratch_shapes=[
            pltpu.VMEM((4 * rows, cols), thin.dtype),
            pltpu.SemaphoreType.DMA((count,)),
            pltpu.SemaphoreType.DMA((count,)),
            pltpu.SemaphoreType.DMA((3,)),
        ],
        compiler_params=pltpu.CompilerParams(collective_id=0, has_side_effects=True),
        name="gather_first",
    )(wide, thin)


def second_gather_kernel(wide_ref, wide_out, send, recv, local):
    greet(gather_peers())
    box = Mailbox(send, recv)
    keep = pltpu.make_async_copy(wide_ref, wide_out.at[moved(0, 0)], local)
    keep.start()
    for step in gather_steps(box, wide_ref, wide_out):
        step()
    keep.wait()
    box.drain()


def second_gather(wide):
    anywhere = pl.BlockSpec(memory_space=pl.ANY)
    return pl.pallas_call(
        second_gather_kernel,
        out_shape=jax.ShapeDtypeStruct((32,) + wide.shape, wide.dtype),
        in_specs=[anywhere],
        out_specs=anywhere,
        scratch_shapes=[
            pltpu.SemaphoreType.DMA((GATHER_COPIES,)),
            pltpu.SemaphoreType.DMA((GATHER_COPIES,)),
            pltpu.SemaphoreType.DMA,
        ],
        compiler_params=pltpu.CompilerParams(collective_id=1, has_side_effects=True),
        name="gather_second",
    )(wide)


def sum_kernel(n_extra, x_ref, *refs):
    if n_extra:
        e_ref, out_ref, e_out, landed, e_landed, send, recv = refs
    else:
        out_ref, landed, send, recv = refs
    m = lax.axis_index("mp")
    rows = x_ref.shape[0] // 2
    width = x_ref.shape[1] // 4
    peers = {k: lax.rem(m + k, 4) for k in (1, 2, 3)}
    greet((), list(peers.values()))
    box = Mailbox(send, recv)

    def columns(i, w):
        return pl.ds(pl.multiple_of(i * w, w), w)

    arriving = []
    for part in range(2):
        r = pl.ds(part * rows, rows)
        arriving.append(
            [
                box.push(x_ref.at[r, columns(peers[k], width)], landed.at[k - 1, r], mp=peers[k])
                for k in (2, 1, 3)
            ]
        )
    if n_extra:
        extra = [
            box.push(e_ref.at[:, columns(peers[k], n_extra)], e_landed.at[k - 1], mp=peers[k])
            for k in (2, 1, 3)
        ]
    gathered = []
    for part in range(2):
        r = pl.ds(part * rows, rows)
        for copy in arriving[part]:
            copy.wait_recv()
        total = x_ref[r, columns(m, width)].astype(WIDE)
        for k in range(3):
            total = total + landed[k, r].astype(WIDE)
        out_ref[r, columns(m, width)] = total.astype(out_ref.dtype)
        block = out_ref.at[r, columns(m, width)]
        gathered += [box.push(block, block, mp=peers[k]) for k in (2, 1, 3)]
    if n_extra:
        for copy in extra:
            copy.wait_recv()
        total = e_ref[:, columns(m, n_extra)].astype(WIDE)
        for k in range(3):
            total = total + e_landed[k].astype(WIDE)
        e_out[...] = total
    for copy in gathered:
        copy.wait_recv()
    box.drain()


def sum_over_mp(x, extra=None, collective_id=0):
    rows, cols = x.shape
    vmem = pl.BlockSpec(memory_space=pltpu.VMEM)
    n_extra = 0 if extra is None else extra.shape[1] // 4
    out_shape = [jax.ShapeDtypeStruct(x.shape, x.dtype)]
    scratch = [pltpu.VMEM((3, rows, cols // 4), x.dtype)]
    count = 12
    if n_extra:
        out_shape.append(jax.ShapeDtypeStruct((rows, n_extra), WIDE))
        scratch.append(pltpu.VMEM((3, rows, n_extra), extra.dtype))
        count += 3
    return pl.pallas_call(
        functools.partial(sum_kernel, n_extra),
        out_shape=tuple(out_shape),
        in_specs=[vmem] * len(out_shape),
        out_specs=tuple([vmem] * len(out_shape)),
        scratch_shapes=scratch
        + [pltpu.SemaphoreType.DMA((count,)), pltpu.SemaphoreType.DMA((count,))],
        compiler_params=pltpu.CompilerParams(
            collective_id=collective_id, has_side_effects=True, vmem_limit_bytes=32 << 20
        ),
        name="sum_over_mp",
    )(*([x] if extra is None else [x, extra]))


def half_dot(left, right, dims=(((1,), (0,)), ((), ()))):
    high = right.astype(NARROW)
    low = (right - high.astype(WIDE)).astype(NARROW)
    return lax.dot_general(left, high, dims, preferred_element_type=WIDE) + lax.dot_general(
        left, low, dims, preferred_element_type=WIDE
    )


TURNED = (((0,), (0,)), ((), ()))


def chain_forward_kernel(
    a_ref, b_ref, state_out, sib_a, chip_a, row_a, sib_b, chip_b, row_b, states, send, recv
):
    y, z, c = coords()
    sibling = moved(0, 0, True)
    z_peers = {k: moved(0, k) for k in (1, 2, 3)}
    y_peers = {k: moved(k, 0) for k in (1, 2, 3)}
    greet([sibling] + list(z_peers.values()) + list(y_peers.values()))
    box = Mailbox(send, recv)
    mine = pl.ds(pl.multiple_of(2 * c, 2), 2)
    theirs = pl.ds(pl.multiple_of(2 * (1 - c), 2), 2)
    pair = [box.push(a_ref.at[theirs], sib_a, dp=sibling), box.push(b_ref.at[theirs], sib_b, dp=sibling)]
    for copy in pair:
        copy.wait_recv()
    first = c == 0
    lower_b = []
    for h in range(2):
        own_a, own_b = a_ref[2 * c + h], b_ref[2 * c + h]
        a_low, a_high = jnp.where(first, own_a, sib_a[h]), jnp.where(first, sib_a[h], own_a)
        b_low, b_high = jnp.where(first, own_b, sib_b[h]), jnp.where(first, sib_b[h], own_b)
        lower_b.append((a_low, b_low))
        chip_a[z, h] = lax.dot(a_high, a_low, preferred_element_type=WIDE).astype(NARROW)
        chip_b[z, h] = (
            lax.dot(a_high, b_low, preferred_element_type=WIDE) + b_high.astype(WIDE)
        ).astype(NARROW)
    ring = []
    for k in (2, 1, 3):
        ring.append(box.push(chip_a.at[z], chip_a.at[z], dp=z_peers[k]))
        ring.append(box.push(chip_b.at[z], chip_b.at[z], dp=z_peers[k]))
    for copy in ring:
        copy.wait_recv()
    for h in range(2):
        total_a, total_b = chip_a[0, h].astype(WIDE), chip_b[0, h].astype(WIDE)
        for i in range(1, 4):
            total_a = half_dot(chip_a[i, h], total_a)
            total_b = half_dot(chip_a[i, h], total_b) + chip_b[i, h].astype(WIDE)
        row_a[y, h] = total_a.astype(NARROW)
        row_b[y, h] = total_b.astype(NARROW)
    column = []
    for k in (2, 1, 3):
        column.append(box.push(row_a.at[y], row_a.at[y], dp=y_peers[k]))
        column.append(box.push(row_b.at[y], row_b.at[y], dp=y_peers[k]))
    for copy in column:
        copy.wait_recv()
    for h in range(2):
        state = jnp.zeros((DH, DH), WIDE)
        for i in range(3):
            longer = half_dot(row_a[i, h], state) + row_b[i, h].astype(WIDE)
            state = jnp.where(i < y, longer, state)
        for i in range(3):
            longer = half_dot(chip_a[i, h], state) + chip_b[i, h].astype(WIDE)
            state = jnp.where(i < z, longer, state)
        a_low, b_low = lower_b[h]
        middle = half_dot(a_low, state) + b_low.astype(WIDE)
        state_out[2 * c + h] = jnp.where(first, state, middle)
        states[h] = jnp.where(first, middle, state)
    back = box.push(states, state_out.at[mine], dp=sibling)
    back.wait_recv()
    box.drain()


def chain_forward(maps, offsets):
    vmem = pl.BlockSpec(memory_space=pltpu.VMEM)
    heads = maps.shape[0]
    two = (2, DH, DH)
    count = 2 + 6 + 6 + 1
    return pl.pallas_call(
        chain_forward_kernel,
        out_shape=(
            jax.ShapeDtypeStruct((heads, DH, DH), WIDE),
            jax.ShapeDtypeStruct(two, NARROW),
            jax.ShapeDtypeStruct((4,) + two, NARROW),
            jax.ShapeDtypeStruct((4,) + two, NARROW),
        ),
        in_specs=[vmem] * 2,
        out_specs=(vmem,) * 4,
        scratch_shapes=[
            pltpu.VMEM(two, NARROW),
            pltpu.VMEM((4,) + two, NARROW),
            pltpu.VMEM((4,) + two, NARROW),
            pltpu.VMEM(two, WIDE),
            pltpu.SemaphoreType.DMA((count,)),
            pltpu.SemaphoreType.DMA((count,)),
        ],
        compiler_params=pltpu.CompilerParams(
            collective_id=4, has_side_effects=True, vmem_limit_bytes=32 << 20
        ),
        name="chain_forward",
    )(maps, offsets)


def chain_backward_kernel(
    a_ref, sib_a, chip_a, row_a, g_ref, grad_out, sib_g, chip_g, row_g, grads, send, recv
):
    y, z, c = coords()
    sibling = moved(0, 0, True)
    z_peers = {k: moved(0, k) for k in (1, 2, 3)}
    y_peers = {k: moved(k, 0) for k in (1, 2, 3)}
    greet([sibling] + list(z_peers.values()) + list(y_peers.values()))
    box = Mailbox(send, recv)
    mine = pl.ds(pl.multiple_of(2 * c, 2), 2)
    theirs = pl.ds(pl.multiple_of(2 * (1 - c), 2), 2)
    box.push(g_ref.at[theirs], sib_g, dp=sibling).wait_recv()
    first = c == 0
    upper = []
    for h in range(2):
        own_a, own_g = a_ref[2 * c + h], g_ref[2 * c + h]
        a_low, a_high = jnp.where(first, own_a, sib_a[h]), jnp.where(first, sib_a[h], own_a)
        g_low, g_high = jnp.where(first, own_g, sib_g[h]), jnp.where(first, sib_g[h], own_g)
        upper.append((a_high, g_high))
        chip_g[z, h] = (
            lax.dot_general(a_low, g_high, TURNED, preferred_element_type=WIDE) + g_low.astype(WIDE)
        ).astype(NARROW)
    ring = [box.push(chip_g.at[z], chip_g.at[z], dp=z_peers[k]) for k in (2, 1, 3)]
    for copy in ring:
        copy.wait_recv()
    for h in range(2):
        total = chip_g[3, h].astype(WIDE)
        for i in (2, 1, 0):
            total = half_dot(chip_a[i, h], total, TURNED) + chip_g[i, h].astype(WIDE)
        row_g[y, h] = total.astype(NARROW)
    column = [box.push(row_g.at[y], row_g.at[y], dp=y_peers[k]) for k in (2, 1, 3)]
    for copy in column:
        copy.wait_recv()
    for h in range(2):
        grad = jnp.zeros((DH, DH), WIDE)
        for i in (3, 2, 1):
            longer = half_dot(row_a[i, h], grad, TURNED) + row_g[i, h].astype(WIDE)
            grad = jnp.where(i > y, longer, grad)
        for i in (3, 2, 1):
            longer = half_dot(chip_a[i, h], grad, TURNED) + chip_g[i, h].astype(WIDE)
            grad = jnp.where(i > z, longer, grad)
        a_high, g_high = upper[h]
        middle = half_dot(a_high, grad, TURNED) + g_high.astype(WIDE)
        grad_out[2 * c + h] = jnp.where(first, middle, grad)
        grads[h] = jnp.where(first, grad, middle)
    box.push(grads, grad_out.at[mine], dp=sibling).wait_recv()
    box.drain()


def chain_backward(maps, kept, offsets):
    vmem = pl.BlockSpec(memory_space=pltpu.VMEM)
    heads = maps.shape[0]
    two = (2, DH, DH)
    count = 1 + 3 + 3 + 1
    return pl.pallas_call(
        chain_backward_kernel,
        out_shape=jax.ShapeDtypeStruct((heads, DH, DH), WIDE),
        in_specs=[vmem] * 5,
        out_specs=vmem,
        scratch_shapes=[
            pltpu.VMEM(two, NARROW),
            pltpu.VMEM((4,) + two, NARROW),
            pltpu.VMEM((4,) + two, NARROW),
            pltpu.VMEM(two, WIDE),
            pltpu.SemaphoreType.DMA((count,)),
            pltpu.SemaphoreType.DMA((count,)),
        ],
        compiler_params=pltpu.CompilerParams(
            collective_id=5, has_side_effects=True, vmem_limit_bytes=32 << 20
        ),
        name="chain_backward",
    )(maps, *kept, offsets)


def wide_dot(left, right, left_dim=1, right_dim=0):
    return lax.dot_general(
        left,
        right,
        (((left_dim,), (right_dim,)), ((), ())),
        precision=EXACT,
        preferred_element_type=WIDE,
    )


def column_of(aux, index):
    lanes = lax.broadcasted_iota(jnp.int32, aux.shape, 1)
    return jnp.sum(jnp.where(lanes == index, aux, 0.0), axis=1, keepdims=True)


def convolve(pre_ref, taps_ref, part, aux, work):
    count = aux.shape[0]
    work[...] = pre_ref[...].astype(WIDE)
    total = work[pl.ds(HALO, count)] * taps_ref[part : part + 1, :]
    for j in range(1, KW):
        total = total + (
            work[pl.ds(HALO - j, count)] * aux[:, j : j + 1] * taps_ref[3 * j + part : 3 * j + part + 1, :]
        )
    return total


def masks(aux, seg_row):
    same = aux[:, 6:7] == seg_row
    shape = (aux.shape[0], aux.shape[0])
    row = lax.broadcasted_iota(jnp.int32, shape, 0)
    col = lax.broadcasted_iota(jnp.int32, shape, 1)
    return row, col, same


def lower_inverse(lower, row, col):
    near = jnp.where(row // 8 == col // 8, lower, 0.0)
    square = wide_dot(near, near)
    inverse = jnp.where(row == col, 1.0, 0.0) - near
    inverse = inverse + wide_dot(inverse, square)
    inverse = inverse + wide_dot(inverse, wide_dot(square, square))
    size = 8
    while size < lower.shape[0]:
        link = jnp.where((row // (2 * size) == col // (2 * size)) & (row // size != col // size), lower, 0.0)
        inverse = inverse - wide_dot(inverse, wide_dot(link, inverse))
        size *= 2
    return inverse


def mixer_forward_kernel(
    q_pre, k_pre, v_pre, taps_ref, aux_ref, seg_ref,
    out_ref, reach_ref, map_ref, offset_ref, q_ref, k_ref, v_ref, t_ref, w_ref, u_ref, work,
):
    head = pl.program_id(0)
    aux = aux_ref[...]
    rate = column_of(aux, 8 + head)
    linked, ending = aux[:, 4:5], aux[:, 5:6]
    row, col, same = masks(aux, seg_ref[0:1, :])
    acts = []
    for part, pre_ref in enumerate((q_pre, k_pre, v_pre)):
        conv = convolve(pre_ref, taps_ref, part, aux, work)
        acts.append(conv * jax.nn.sigmoid(conv))
    q = acts[0] * lax.rsqrt(jnp.sum(acts[0] * acts[0], axis=1, keepdims=True) + EPSILON)
    k = acts[1] * lax.rsqrt(jnp.sum(acts[1] * acts[1], axis=1, keepdims=True) + EPSILON)
    v = acts[2]
    q_ref[...] = q
    k_ref[...] = k
    v_ref[...] = v
    gram = wide_dot(k, k, 1, 1)
    inverse = lower_inverse(jnp.where((row > col) & same, gram * rate, 0.0), row, col)
    t_ref[0] = inverse
    written = wide_dot(inverse, jnp.concatenate([v, k * linked], axis=1) * rate)
    w_ref[...] = written[:, :DH]
    u_ref[...] = written[:, DH:]
    scores = jnp.where((row >= col) & same, wide_dot(q, k, 1, 1), 0.0)
    mixed = wide_dot(scores, written)
    out_ref[...] = mixed[:, :DH]
    reach_ref[...] = q * linked - mixed[:, DH:]
    ends = wide_dot(k * ending, written, 0, 0)
    offset_ref[0] = ends[:, :DH].astype(offset_ref.dtype)
    eye = jnp.where(row[:DH, :DH] == col[:DH, :DH], 1.0, 0.0)
    last = aux[aux.shape[0] - 1 :, 4:5]
    map_ref[0] = (eye * last - ends[:, DH:]).astype(map_ref.dtype)


def mixer_forward(pre, taps, aux, seg_row):
    count = aux.shape[0]
    heads = pre.shape[1] // (3 * DH)

    def part(p):
        return pl.BlockSpec((pre.shape[0], DH), lambda h: (0, p * heads + h))

    whole = lambda x: pl.BlockSpec(x.shape, lambda h: (0,) * x.ndim)
    by_head = pl.BlockSpec((count, DH), lambda h: (0, h))
    square = lambda n: pl.BlockSpec((1, n, n), lambda h: (h, 0, 0))
    wide = jax.ShapeDtypeStruct((count, heads * DH), WIDE)
    small = jax.ShapeDtypeStruct((heads, DH, DH), NARROW)
    return pl.pallas_call(
        mixer_forward_kernel,
        grid=(heads,),
        out_shape=(wide, wide, small, small, wide, wide, wide,
                   jax.ShapeDtypeStruct((heads, count, count), WIDE), wide, wide),
        in_specs=[part(0), part(1), part(2), pl.BlockSpec((16, DH), lambda h: (0, h)), whole(aux), whole(seg_row)],
        out_specs=(by_head, by_head, square(DH), square(DH), by_head, by_head, by_head, square(count), by_head, by_head),
        scratch_shapes=[pltpu.VMEM((pre.shape[0], DH), WIDE)],
        compiler_params=pltpu.CompilerParams(vmem_limit_bytes=40 << 20),
        name="mixer_forward",
    )(pre, pre, pre, taps, aux, seg_row)


def mixer_backward_kernel(
    q_pre, k_pre, v_pre, taps_ref, aux_ref, seg_ref,
    q_ref, k_ref, v_ref, t_ref, w_ref, u_ref, state_ref, grad_ref, d_out_ref,
    dq_pre, dk_pre, dv_pre, d_rate_ref, work,
):
    head = pl.program_id(0)
    aux = aux_ref[...]
    count = aux.shape[0]
    rate = column_of(aux, 8 + head)
    linked, ending = aux[:, 4:5], aux[:, 5:6]
    row, col, same = masks(aux, seg_ref[0:1, :])
    q, k, v = q_ref[...], k_ref[...], v_ref[...]
    state, grad, d_out = state_ref[0], grad_ref[0], d_out_ref[...]
    written = w_ref[...] - wide_dot(u_ref[...], state)
    upto = (row >= col) & same
    scores = jnp.where(upto, wide_dot(q, k, 1, 1), 0.0)
    d_written = wide_dot(scores, d_out, 0, 0) + wide_dot(k * ending, grad)
    d_scores = jnp.where(upto, wide_dot(d_out, written, 1, 1), 0.0)
    d_q = wide_dot(d_scores, k) + linked * wide_dot(d_out, state, 1, 1)
    d_k = wide_dot(d_scores, q, 0, 0) + ending * wide_dot(written, grad, 1, 1)
    d_right = wide_dot(t_ref[0], d_written, 0, 0)
    d_v = rate * d_right
    d_rate = jnp.sum(d_right * (v - linked * wide_dot(k, state)), axis=1, keepdims=True)
    d_k = d_k - (linked * rate) * wide_dot(d_right, state, 1, 1)
    d_lower = jnp.where((row > col) & same, -wide_dot(d_right, written, 1, 1), 0.0)
    d_rate = d_rate + jnp.sum(d_lower * wide_dot(k, k, 1, 1), axis=1, keepdims=True)
    d_gram = d_lower * rate
    d_k = d_k + wide_dot(d_gram, k) + wide_dot(d_gram, k, 0, 0)

    @pl.when(head == 0)
    def _():
        d_rate_ref[...] = jnp.zeros_like(d_rate_ref)

    lanes = lax.broadcasted_iota(jnp.int32, aux.shape, 1)
    d_rate_ref[...] += jnp.where(lanes == head, d_rate, 0.0)
    for part, (pre_ref, out_ref, unit, d) in enumerate(
        ((q_pre, dq_pre, q, d_q), (k_pre, dk_pre, k, d_k), (v_pre, dv_pre, None, d_v))
    ):
        conv = convolve(pre_ref, taps_ref, part, aux, work)
        gate = jax.nn.sigmoid(conv)
        if unit is not None:
            act = conv * gate
            scale = lax.rsqrt(jnp.sum(act * act, axis=1, keepdims=True) + EPSILON)
            d = (d - unit * jnp.sum(unit * d, axis=1, keepdims=True)) * scale
        d_conv = d * gate * (1.0 + conv * (1.0 - gate))
        out_ref[...] = jnp.zeros_like(out_ref)
        for j in range(KW):
            term = d_conv * taps_ref[3 * j + part : 3 * j + part + 1, :]
            if j:
                term = term * aux[:, j : j + 1]
            out_ref[pl.ds(HALO - j, count)] += term


def mixer_backward(pre, taps, aux, seg_row, kept, state, grad, d_out):
    count = aux.shape[0]
    heads = pre.shape[1] // (3 * DH)

    def part(p):
        return pl.BlockSpec((pre.shape[0], DH), lambda h: (0, p * heads + h))

    whole = lambda x: pl.BlockSpec(x.shape, lambda h: (0,) * x.ndim)
    by_head = pl.BlockSpec((count, DH), lambda h: (0, h))
    long_by_head = pl.BlockSpec((pre.shape[0], DH), lambda h: (0, h))
    square = lambda n: pl.BlockSpec((1, n, n), lambda h: (h, 0, 0))
    wide = jax.ShapeDtypeStruct((pre.shape[0], heads * DH), WIDE)
    return pl.pallas_call(
        mixer_backward_kernel,
        grid=(heads,),
        out_shape=(wide, wide, wide, jax.ShapeDtypeStruct(aux.shape, WIDE)),
        in_specs=[part(0), part(1), part(2), pl.BlockSpec((16, DH), lambda h: (0, h)), whole(aux), whole(seg_row),
                  by_head, by_head, by_head, square(count), by_head, by_head, square(DH), square(DH), by_head],
        out_specs=(long_by_head, long_by_head, long_by_head, whole(aux)),
        scratch_shapes=[pltpu.VMEM((pre.shape[0], DH), WIDE)],
        compiler_params=pltpu.CompilerParams(vmem_limit_bytes=40 << 20),
        name="mixer_backward",
    )(pre, pre, pre, taps, aux, seg_row, *kept, state, grad, d_out)


def inverse_rms(values):
    return lax.rsqrt(jnp.mean(values * values, axis=-1, keepdims=True) + EPSILON)


def norm_back(values, scale, gain, grad_out):
    weighted = grad_out * gain
    return scale * weighted - values * scale**3 * jnp.mean(weighted * values, axis=-1, keepdims=True)


def dot(left, right):
    return jnp.dot(left, right, preferred_element_type=WIDE)


def dot_nt(left, right):
    return lax.dot_general(left, right, (((1,), (1,)), ((), ())), preferred_element_type=WIDE)


def dot_tn(left, right):
    return lax.dot_general(left, right, (((0,), (0,)), ((), ())), preferred_element_type=WIDE)


def shifted(value, steps):
    count = lax.axis_size("dp")
    pairs = [(i, i + steps) for i in range(max(0, -steps), min(count, count - steps))]
    return lax.ppermute(value, "dp", pairs)


def pack_ranks(ranks, blocks):
    flat = ranks.reshape(-1, 128)
    flat = jnp.pad(flat, ((0, 64 * blocks - flat.shape[0]), (0, 0)))
    return flat.reshape(blocks, 64, 128).transpose(1, 0, 2).reshape(64, blocks * 128)


def unpack_ranks(packed, tiles):
    blocks = packed.shape[2] // 128
    flat = packed.reshape(32, 64, blocks, 128).transpose(0, 2, 1, 3).reshape(32, 64 * blocks, 128)
    return flat[:, : 4 * tiles].reshape(128, tiles * 128)


def on_device(
    layer_in, cotangent, segments, adapters, norm_one, norm_two, out_gain, beta_bias, conv_taps,
    w_qkv, w_beta, w_out, w_gate_up, w_down, a_in, b_heads, b_beta, a_out, b_ffn, a_down, b_res,
):
    count = layer_in.shape[0]
    m = lax.axis_index("mp")
    heads = w_beta.shape[1]
    inner = heads * DH
    ff = w_down.shape[0]

    pad_beta = jnp.pad(w_beta, ((0, 0), (0, 128 - heads)))
    ranks_one = pack_ranks(
        jnp.concatenate(
            [b_heads.transpose(1, 0, 2).reshape(4, 3 * inner), jnp.pad(b_beta, ((0, 0), (0, 128 - heads)))],
            axis=1,
        ),
        1,
    )
    wide_one = jnp.concatenate([w_qkv.reshape(64, 3 * inner), pad_beta, ranks_one], axis=1)
    thin_one = jnp.concatenate([a_in.reshape(16, 768), b_res.transpose(2, 0, 1).reshape(16, 256)], axis=1)
    ranks_two = pack_ranks(
        jnp.concatenate([b_ffn.transpose(1, 0, 2).reshape(4, 2 * ff), a_out.T, a_down.T], axis=1), 3
    )
    wide_two = jnp.concatenate([w_out.T, w_gate_up.reshape(64, 2 * ff), w_down.T, ranks_two], axis=1)
    full_one, full_thin = first_gather(wide_one, thin_one)
    wide_two, full_one, full_thin = lax.optimization_barrier((wide_two, full_one, full_thin))
    full_two = second_gather(wide_two)

    ranks = unpack_ranks(full_one[:, :, 3 * inner + 128 :], 13)
    full_one = full_one.reshape(2048, -1)
    w_qkv_full = full_one[:, : 3 * inner]
    w_beta_full = full_one[:, 3 * inner : 3 * inner + 128]
    b_heads_full = [ranks[:, j * inner : (j + 1) * inner] for j in range(3)]
    b_beta_full = ranks[:, 3 * inner :]
    full_thin = full_thin.reshape(2048, 1024)
    a_one, a_two = full_thin[:, :512], full_thin[:, 512:768]
    b_res_mix, b_res_down = full_thin[:, 768:896], full_thin[:, 896:]

    ranks = unpack_ranks(full_two[:, :, inner + 3 * ff :], 37)
    full_two = full_two.reshape(2048, -1)
    w_out_full = full_two[:, :inner]
    w_gate_up_full = full_two[:, inner : inner + 2 * ff]
    w_down_full = full_two[:, inner + 2 * ff : inner + 3 * ff]
    b_ffn_full = [ranks[:, j * ff : (j + 1) * ff] for j in range(2)]
    a_out_full = ranks[:, 2 * ff : 2 * ff + inner]
    a_down_full = ranks[:, 2 * ff + inner :]

    before_rows = shifted(layer_in[count - HALO :], 1)
    before_ids = shifted(segments[count - HALO :] + 1, 1) - 1
    rows_ext = jnp.concatenate([before_rows, layer_in]).astype(WIDE)
    seg_ext = jnp.concatenate([before_ids, segments])
    seg_count = adapters.shape[0]
    per_token = jnp.sum(
        jnp.where(seg_ext[:, None] == jnp.arange(seg_count, dtype=jnp.int32)[None, :], adapters[None, :], 0), axis=1
    )
    owner_ids = jnp.arange(128, dtype=jnp.int32) // RANK
    picks_ext = (per_token[:, None] == owner_ids[None, :]).astype(WIDE)
    picks = picks_ext[HALO:]
    same = [
        (seg_ext[HALO - j : HALO - j + count] == segments).astype(WIDE) for j in range(KW)
    ]
    seg_float = segments.astype(WIDE)
    g_full = lax.all_gather(cotangent, "mp", axis=1, tiled=True)

    scale_ext = inverse_rms(rows_ext)
    xn_ext = (rows_ext * scale_ext * norm_one).astype(NARROW)
    u_ext = (dot(xn_ext, a_one) * jnp.tile(picks_ext, (1, 4))).astype(NARROW)
    pre = (
        dot(xn_ext, w_qkv_full)
        + jnp.concatenate([dot(u_ext[:, j * 128 : (j + 1) * 128], b_heads_full[j]) for j in range(3)], axis=1)
    ).astype(NARROW)
    xn_one, u_one = xn_ext[HALO:], u_ext[HALO:]
    logits = dot(xn_one, w_beta_full) + dot(u_one[:, 384:], b_beta_full)
    strength = jax.nn.sigmoid(logits[:, :heads] + beta_bias)
    aux = jnp.concatenate(
        [s[:, None] for s in same]
        + [
            (segments == before_ids[HALO - 1]).astype(WIDE)[:, None],
            (segments == segments[count - 1]).astype(WIDE)[:, None],
            seg_float[:, None],
            jnp.zeros((count, 1), WIDE),
            strength,
            jnp.zeros((count, 128 - 8 - heads), WIDE),
        ],
        axis=1,
    )
    seg_row = jnp.broadcast_to(seg_float[None, :], (8, count))
    taps = jnp.pad(conv_taps.reshape(3 * KW, inner).astype(WIDE), ((0, 4), (0, 0)))
    out_zero, reach, maps, offsets, *kept = mixer_forward(pre, taps, aux, seg_row)
    state_in, *kept_maps = chain_forward(maps, offsets)
    by_head = lambda x: x.reshape(count, heads, DH)
    mixer_out = by_head(out_zero) + jnp.einsum(
        "thk,hkv->thv", by_head(reach), state_in, precision=EXACT
    )
    mixer_scale = inverse_rms(mixer_out)
    normed = (mixer_out * mixer_scale * out_gain).astype(NARROW).reshape(count, inner)
    u_out = dot_nt(normed, a_out_full) * picks
    u_out_narrow = u_out.astype(NARROW)
    branch_part = dot_nt(normed, w_out_full) + dot_nt(u_out_narrow, b_res_mix)
    (branch,) = sum_over_mp(branch_part.astype(NARROW), collective_id=2)

    rows = rows_ext[HALO:]
    hidden_one = rows + branch.astype(WIDE)
    scale_two = inverse_rms(hidden_one)
    xn_two = (hidden_one * scale_two * norm_two).astype(NARROW)
    u_two = (dot(xn_two, a_two) * jnp.tile(picks, (1, 2))).astype(NARROW)
    gate_up = dot(xn_two, w_gate_up_full) + jnp.concatenate(
        [dot(u_two[:, j * 128 : (j + 1) * 128], b_ffn_full[j]) for j in range(2)], axis=1
    )
    gate, up = gate_up[:, :ff], gate_up[:, ff:]
    sig = jax.nn.sigmoid(gate)
    hidden = (gate * sig * up).astype(NARROW)
    u_down = (dot_nt(hidden, a_down_full) * picks).astype(NARROW)
    ffn_part = dot_nt(hidden, w_down_full) + dot_nt(u_down, b_res_down)
    ffn_share = lax.psum_scatter(ffn_part.astype(NARROW), "mp", scatter_dimension=1, tiled=True)
    share = ffn_share.shape[1]
    start_col = m * share
    output = (
        lax.dynamic_slice_in_dim(hidden_one, start_col, share, 1) + ffn_share.astype(WIDE)
    ).astype(NARROW)

    g_wide = g_full.astype(WIDE)
    e_down = (dot(g_full, b_res_down) * picks).astype(NARROW)
    grad_a_down = dot_tn(e_down, hidden)
    d_hidden = dot(g_full, w_down_full) + dot(e_down, a_down_full)
    d_gate = d_hidden * up * sig * (1.0 + gate * (1.0 - sig))
    d_up = d_hidden * gate * sig
    d_gate_up = jnp.concatenate([d_gate, d_up], axis=1).astype(NARROW)
    e_two = jnp.concatenate(
        [dot_nt(d_gate_up[:, j * ff : (j + 1) * ff], b_ffn_full[j]) * picks for j in range(2)], axis=1
    ).astype(NARROW)
    grad_b_ffn = jnp.concatenate(
        [dot_tn(u_two[:, j * 128 : (j + 1) * 128], d_gate_up[:, j * ff : (j + 1) * ff]) for j in range(2)], axis=1
    )
    d_xn_two_part = dot_nt(d_gate_up, w_gate_up_full) + dot_nt(e_two, a_two)
    extra = jnp.concatenate([e_two, u_out_narrow, u_down], axis=1)
    d_xn_two, shared_two = sum_over_mp(d_xn_two_part.astype(NARROW), extra, collective_id=3)
    d_hidden_one = g_wide + norm_back(hidden_one, scale_two, norm_two, d_xn_two.astype(WIDE))

    d_branch = d_hidden_one.astype(NARROW)
    e_out = (dot(d_branch, b_res_mix) * picks).astype(NARROW)
    grad_a_out = dot_tn(e_out, normed)
    d_normed = dot(d_branch, w_out_full) + dot(e_out, a_out_full)
    d_mixer = norm_back(mixer_out, mixer_scale, out_gain, by_head(d_normed))
    d_state = jnp.einsum("thk,thv->hkv", by_head(reach), d_mixer, precision=EXACT)
    state_grad = chain_backward(maps, kept_maps, d_state.astype(NARROW))
    dq_pre, dk_pre, dv_pre, d_rate = mixer_backward(
        pre, taps, aux, seg_row, kept, state_in, state_grad, d_mixer.reshape(count, inner)
    )
    d_pre_ext = jnp.concatenate([dq_pre, dk_pre, dv_pre], axis=1)
    from_next = shifted(d_pre_ext[HALO - KW + 1 : HALO], -1)
    d_pre = d_pre_ext[HALO:].at[count - KW + 1 :].add(from_next).astype(NARROW)
    d_logit = (d_rate[:, :heads] * strength * (1.0 - strength)).astype(NARROW)
    d_logit_pad = jnp.pad(d_logit, ((0, 0), (0, 128 - heads)))
    e_one = (
        jnp.concatenate(
            [dot_nt(d_pre[:, j * inner : (j + 1) * inner], b_heads_full[j]) for j in range(3)]
            + [dot_nt(d_logit_pad, b_beta_full)],
            axis=1,
        )
        * jnp.tile(picks, (1, 4))
    ).astype(NARROW)
    grad_b_heads = jnp.concatenate(
        [dot_tn(u_one[:, j * 128 : (j + 1) * 128], d_pre[:, j * inner : (j + 1) * inner]) for j in range(3)], axis=1
    )
    grad_b_beta = dot_tn(u_one[:, 384:], d_logit)
    d_xn_one_part = dot_nt(d_pre, w_qkv_full) + dot_nt(d_logit_pad, w_beta_full) + dot_nt(e_one, a_one)
    d_xn_one, shared_one = sum_over_mp(d_xn_one_part.astype(NARROW), e_one, collective_id=6)
    grad_full = d_hidden_one + norm_back(rows, scale_ext[HALO:], norm_one, d_xn_one.astype(WIDE))
    grad_input = lax.dynamic_slice_in_dim(grad_full, start_col, share, 1)

    left_two = jnp.where(m < 2, xn_two, jnp.where(m == 2, d_branch, g_full))
    shared_two = dot_tn(left_two, shared_two.astype(NARROW))
    shared_one = dot_tn(xn_one, shared_one.astype(NARROW))

    def rank_rows(x):
        return x.reshape(32, 4, -1)

    early = jnp.concatenate(
        [rank_rows(x).reshape(32, -1, 128) for x in (grad_b_ffn, grad_a_out, grad_a_down)]
        + [shared_two.reshape(32, 64, 128)],
        axis=1,
    ).astype(NARROW)
    early = lax.psum_scatter(early, "dp", scatter_dimension=0, tiled=True)[0].astype(WIDE)
    late = jnp.concatenate(
        [
            rank_rows(grad_b_heads).reshape(32, -1, 128),
            jnp.pad(rank_rows(grad_b_beta), ((0, 0), (0, 0), (0, 128 - heads))),
            shared_one.reshape(32, 64, 128),
        ],
        axis=1,
    ).astype(NARROW)
    late = jnp.sum(lax.all_to_all(late, "dp", 0, 0, tiled=True).astype(WIDE), axis=0)
    shared = jnp.stack([late[-64:].reshape(4, 16, 128), early[-64:].reshape(4, 16, 128)], axis=1)
    shared = lax.all_to_all(shared, "mp", 0, 0, tiled=True)
    out_grad_a_in = jnp.concatenate(
        [shared[j, 0][:, None] for j in range(4)] + [shared[j, 1][:, None] for j in range(2)], axis=1
    )
    out_grad_b_res = jnp.stack([shared[2, 1].T, shared[3, 1].T])
    n_ffn, n_out, n_down = 2 * ff * 4 // 128, inner * 4 // 128, ff * 4 // 128
    out_b_ffn = early[:n_ffn].reshape(4, 2, ff).transpose(1, 0, 2)
    out_a_out = early[n_ffn : n_ffn + n_out].reshape(4, inner).T
    out_a_down = early[n_ffn + n_out : n_ffn + n_out + n_down].reshape(4, ff).T
    n_heads = 3 * inner * 4 // 128
    out_b_heads = late[:n_heads].reshape(4, 3, inner).transpose(1, 0, 2)
    out_b_beta = late[n_heads : n_heads + 4, :heads]
    return (
        output, grad_input, out_grad_a_in, out_b_heads, out_b_beta, out_a_out, out_b_ffn, out_a_down, out_grad_b_res,
    )


def solution(mesh):
    placed = (
        P("dp", None),
        P("dp", "mp"),
        P("dp"),
        P(),
        P(),
        P(),
        P(),
        P("mp"),
        P(None, None, "mp"),
        P("dp", None, "mp"),
        P("dp", "mp"),
        P("mp", "dp"),
        P("dp", None, "mp"),
        P("mp", "dp"),
        P(("dp", "mp"), None, None),
        P(None, "dp", "mp"),
        P("dp", "mp"),
        P("mp", "dp"),
        P(None, "dp", "mp"),
        P("mp", "dp"),
        P(None, None, ("dp", "mp")),
    )
    return jax.shard_map(
        on_device,
        mesh=mesh,
        in_specs=placed,
        out_specs=(
            P("dp", "mp"),
            P("dp", "mp"),
            P(("dp", "mp"), None, None),
            P(None, "dp", "mp"),
            P("dp", "mp"),
            P("mp", "dp"),
            P(None, "dp", "mp"),
            P("mp", "dp"),
            P(None, None, ("dp", "mp")),
        ),
        check_vma=False,
    )
```

time: 2170 us -> 510 us (0.24)
  waiting for transfers between devices: 800 us -> 13.3 us
  blocking collectives: 415 us -> 0 us
  matrix products: 443 us -> 82.8 us
  other arithmetic: 320 us -> 25.9 us
  Pallas kernels: 0 us -> 291 us
  local copies, waits for them, and re-layouts: 136 us -> 54.5 us
    all_gather x19 -> x1, waiting for transfers between devices: 458 us -> 0.01 us  [on_device(): g_full = lax.all_gather(cotangent, 'mp', axis=1, tiled=True)]
    dot_general x311 -> x46, matrix products: 429 us -> 82.8 us  [the longest x17 34.7 us: dot_nt(): lax.dot_general(left, right, (((1,), (1,)), ((), ())), preferred_element_...]
    all_gather x12 -> x0, blocking collectives: 294 us -> none  [the longest x2 54.1 us: fetch_weights(): lax.all_gather(a_down, 'dp', axis=1, tiled=True)]
    pallas_call x0 -> x9, Pallas kernels: none -> 291 us  [the longest x3 91.8 us: sum_over_mp(): pl.pallas_call(functools.partial(sum_kernel, n_extra), out_shape=tuple(ou...]
    another operation x66 -> x2, other arithmetic: 241 us -> 1.25 us  [the longest x1 0.64 us: on_device(): jnp.stack([late[-64:].reshape(4, 16, 128), early[-64:].reshape(4, 16, 128...]
    reduce_scatter x2 -> x1, waiting for transfers between devices: 215 us -> 0.01 us  [on_device(): lax.psum_scatter(ffn_part.astype(NARROW), 'mp', scatter_dimension=1, tile...]
    unnamed x1 -> x0, blocking collectives: 121 us -> none
    psum x3 -> x0, waiting for transfers between devices: 121 us -> none  [the longest x1 79.2 us: forward_pass(): branch = lax.psum(partial_mix, 'mp')]
  transfers between devices with their start and end apart: 30 -> 8, of which waited for: 17 -> 1; matrix products, arithmetic and copies ran while one was open for 34% -> 19% of each run, Pallas kernels for 0% -> 52%
where the time goes in v1:
time: 510 us; the launch traced here: 501 us
  Pallas kernels  291 us (57%)
  matrix products  82.8 us (16%)
  local copies, waits for them, and re-layouts  54.5 us (11%)
  other arithmetic  25.9 us (5%)
  starting transfers between devices  17.7 us (3%)
  between operations  15.9 us (3%)
  waiting for transfers between devices  13.3 us (3%)
    pallas_call x3, Pallas kernels, sum_over_mp(): pl.pallas_call(functools.partial(sum_kernel, n_extra), out_shape=tuple(ou...  91.8 us
    pallas_call x1, Pallas kernels, second_gather(): pl.pallas_call(second_gather_kernel, out_shape=jax.ShapeDtypeStruct((32,)...  61.7 us
    pallas_call x1, Pallas kernels, first_gather(): pl.pallas_call(first_gather_kernel, out_shape=(jax.ShapeDtypeStruct((32,)...  40.9 us
    pallas_call x1, Pallas kernels, mixer_forward(): pl.pallas_call(mixer_forward_kernel, grid=(heads,), out_shape=(wide, wide...  36.5 us
    dot_general x17, matrix products, dot_nt(): lax.dot_general(left, right, (((1,), (1,)), ((), ())), preferred_element_...  34.7 us
    dot_general x17, matrix products, dot(): return jnp.dot(left, right, preferred_element_type=WIDE)  33.2 us
    pallas_call x1, Pallas kernels, chain_forward(): pl.pallas_call(chain_forward_kernel, out_shape=(jax.ShapeDtypeStruct((hea...  23.3 us
    pallas_call x1, Pallas kernels, mixer_backward(): pl.pallas_call(mixer_backward_kernel, grid=(heads,), out_shape=(wide, wid...  18.5 us
  transfers between devices with their start and end apart: 8, of which 1 were waited for; matrix products, arithmetic and copies ran while one was open for 19% of the time, Pallas kernels for 52%

profile of v1, /device:TPU:1, one launch (start us, length us, event | category | flops | bytes accessed | tf_op | source)
XLA Modules:
  0.0 500.8 jit_solution(1247201522033323283)
XLA Ops:
  8.1 4.9 collective-permute-start.1
  24.9 40.9 %gather_first.1 = (bf16[32,64,1792]{2,1,0:T(8,128)(2,1)}, bf16[32,64,1024]{2,1,0:T(8,128)(2,1)}) custom-call(bf16[64,1792]{1,0:T(8,128)(2,1)} %fusion.109.wide_ref, bf16[16,1024]{1,0:T(8,128)(2,1)} %pad_maximum_fusion.7.thin_ref), custom_call_target="tpu_custom_call" | custom-call | tf_op jit(solution)/shard_map/gather_first/pallas_call | solution.py:192
  68.5 61.7 %gather_second.1 = bf16[32,64,5120]{2,1,0:T(8,128)(2,1)} custom-call(bf16[64,5120]{1,0:T(8,128)(2,1)} %pad_maximum_fusion.2.wide_ref), custom_call_target="tpu_custom_call" | custom-call | tf_op jit(solution)/shard_map/gather_second/pallas_call | solution.py:224
  146.4 4.7 fusion.24.q_pre.k_pre.v_pre
  151.9 36.5 %mixer_forward.1 = (f32[256,512]{1,0:T(8,128)S(1)}, f32[256,512]{1,0:T(8,128)S(1)}, bf16[4,128,128]{2,1,0:T(8,128)(2,1)S(1)}, bf16[4,128,128]{2,1,0:T(8,128)(2,1...) custom-call(bf16[272,1536]{1,0:T(8,128)(2,1)S(1)} %fusion.24.q_pre.k, ...), custom_call_target="tpu_custom_call" | custom-call | tf_op jit(solution)/shard_map/mixer_forward/pallas_call | solution.py:588
  197.7 23.3 %chain_forward.1 = (f32[4,128,128]{2,1,0:T(8,128)S(1)}, bf16[2,128,128]{2,1,0:T(8,128)(2,1)S(1)}, bf16[4,2,128,128]{3,2,1,0:T(8,128)(2,1)S(1)}, bf16[4,2,128,128]{3,2,1,0:T(8,128)(2,1)S(1)}) custom-call(bf16[4,128,128]{2,1,0:T(8,128)(2,1)S(1)} %get-tuple-element.53.a_ref, bf16[4,128,128]{2,1,0:T(8,128)(2,1)S(1)} %copy-done.17), custom_call_target="tpu_custom_call" | custom-call | tf_op jit(solution)/shard_map/chain_forward/pallas_call | solution.py:393
  228.5 26.4 %sum_over_mp.3 = bf16[256,2048]{1,0:T(8,128)(2,1)S(1)} custom-call(bf16[256,2048]{1,0:T(8,128)(2,1)S(1)} %fusion.30.x_ref), custom_call_target="tpu_custom_call" | custom-call | tf_op jit(solution)/shard_map/sum_over_mp/pallas_call | solution.py:302
  260.4 9.1 %fusion.12 = f32[256,2816]{1,0:T(8,128)} fusion(bf16[256,2048]{1,0:T(8,128)(2,1)S(1)} %multiply_convert_fusion.1, bf16[2048,5120]{1,0:T(8,128)(2,1)} %bitcast.154, f32[256,1408]{1,0:T(8,128)S(1)} %fusion.94, f32[256,1408]{1,0:T(8,128)S(1)} %fusion.97), kind=kOutput, calls=%fused_computation.12 | convolution fusion | flops 2954231808 | bytes 18350080 | tf_op jit(solution)/shard_map/dot_general | solution.py:689
  271.4 4.9 fusion.18
  279.6 9.6 %fusion = f32[256,2048]{1,0:T(8,128)} fusion(bf16[2048,5120]{1,0:T(8,128)(2,1)} %bitcast.156, bf16[256,1408]{1,0:T(8,128)(2,1)} %copy-done.42, bf16[256,1408]{1,0:T(8,128)(2,1)} %copy-done.43), kind=kOutput, calls=%fused_computation | convolution fusion | flops 2955673600 | bytes 15073280 | tf_op jit(solution)/shard_map/dot_general | solution.py:693
  297.0 29.2 %sum_over_mp.4 = (bf16[256,2048]{1,0:T(8,128)(2,1)S(1)}, f32[256,128]{1,0:T(8,128)S(1)}) custom-call(bf16[256,2048]{1,0:T(8,128)(2,1)S(1)} %fusion.35.x_ref, bf16[256,512]{1,0:T(8,128)(2,1)S(1)} %pad_maximum_fusion.4.refs_0_), custom_call_target="tpu_custom_call" | custom-call | tf_op jit(solution)/shard_map/sum_over_mp/pallas_call | solution.py:302
  327.3 2.6 fusion.63
  339.1 2.7 reshape_reshape.17
  344.7 3.0 convolution_convert_fusion
  357.3 18.0 %chain_backward.1.grad_ref = f32[4,128,128]{2,1,0:T(8,128)S(1)} custom-call(bf16[4,128,128]{2,1,0:T(8,128)(2,1)S(1)} %get-tuple-element.53.a_ref, bf16[2,128,128]{2,1,0:T(8,128)(2,1)S(1)} %copy-done.19, bf16[4,2,128,128]{3,2,1,0:T(8,128)(2,1)S(1)} %copy-done.13, bf16[4,2,128,128]{3,2,1,0:T(8,128)(2,1)S(1)} %copy-done.15, ...), custom_call_target="tpu_custom_call" | custom-call | tf_op jit(solution)/shard_map/chain_backward/pallas_call | solution.py:472
  375.3 18.5 %mixer_backward.1 = (f32[272,512]{1,0:T(8,128)S(1)}, f32[272,512]{1,0:T(8,128)S(1)}, f32[272,512]{1,0:T(8,128)S(1)}, f32[256,128]{1,0:T(8,128)S(1)}) custom-call(bf16[272,1536]{1,0:T(8,128)(2,1)S(1)} %fusion.24.q_pre.k_pre.v_pre, bf16[272,1536]{1,0:T(8,128)(2,1)S(1)} %fusion.24.q_pre.k_pre.v_pre, bf16[272,1536]{1,0:T(8,128)(2,1)S(1)} %fusion.24.q_pre.k_pre.v_pre, ...), custom_call_target="tpu_custom_call" | custom-call | tf_op jit(solution)/shard_map/mixer_backward/pallas_call | solution.py:666
  396.4 2.8 fusion.85
  399.3 4.5 fusion.10
  403.8 2.5 fusion.34
  413.0 4.7 fusion.31.x_ref
  420.1 36.2 %sum_over_mp.5 = (bf16[256,2048]{1,0:T(8,128)(2,1)S(1)}, f32[256,128]{1,0:T(8,128)S(1)}) custom-call(bf16[256,2048]{1,0:T(8,128)(2,1)S(1)} %fusion.31.x_ref, bf16[256,512]{1,0:T(8,128)(2,1)S(1)} %fusion.77.refs_0_), custom_call_target="tpu_custom_call" | custom-call | tf_op jit(solution)/shard_map/sum_over_mp/pallas_call | solution.py:302
  458.0 4.4 all-to-all-start
  465.3 13.3 %all-to-all-done = bf16[32,116,128]{2,1,0:T(8,128)(2,1)} async-done(((bf16[32,116,128]{2,1,0:T(8,128)(2,1)}), bf16[32,116,128]{2,1,0:T(8,128)(2,1)}, u32[]{:S(2)}, u32[]{:S(2)}) %all-to-all-start) | async-done | bytes 950304 | tf_op jit(solution)/shard_map/all_to_all | solution.py:910
  482.6 4.1 all-to-all-start.1
  (336 shorter events, 116.4 us)
Async XLA Ops:
  7.2 58.6 %copy-start.67 = (bf16[512,64]{0,1:T(8,128)(2,1)S(1)}, bf16[512,64]{0,1:T(8,128)(2,1)}, u32[]{:S(2)}) copy-start(bf16[512,64]{0,1:T(8,128)(2,1)} %param.34) | copy-start | bytes 196612
  7.2 58.6 %copy-start.65 = (bf16[1408,64]{0,1:T(8,128)(2,1)S(1)}, bf16[1408,64]{0,1:T(8,128)(2,1)}, u32[]{:S(2)}) copy-start(bf16[1408,64]{0,1:T(8,128)(2,1)} %param.36) | copy-start | bytes 540676
  7.2 262.3 %all-gather.2.cloned.1.call-start = ((), (), s32[]{:S(2)}) async-start(), calls=%async_computation.5 | async-start | bytes 1310720 | tf_op jit(solution)/shard_map/all_gather | solution.py:780
  8.1 129.9 %collective-permute-start.1 = (s32[16]{0:T(128)S(1)}, s32[16]{0:T(128)S(1)}, u32[]{:S(2)}, u32[]{:S(2)}) collective-permute-start(s32[16]{0:T(128)S(1)} %slice_add_fusion.2), channel_id=1, source_target_pairs={{0,4},{4,8},{8,12},{12,16},{16,20},{20,24},{24,28},{28,32},{32,36}... | collective-permute-start | bytes 200 | tf_op jit(solution)/shard_map/ppermute | solution.py:703
  14.5 127.2 %collective-permute-start = (bf16[16,2048]{1,0:T(8,128)(2,1)}, bf16[16,2048]{1,0:T(8,128)(2,1)S(1)}, u32[]{:S(2)}, u32[]{:S(2)}) collective-permute-start(bf16[16,2048]{1,0:T(8,128)(2,1)} %slice.240), channel_id=1, source_target_pairs={{0,4},{4,8},{8,12},{12,16},{16,20},{20,24},{24,28},{28,32},{32,36}... | collective-permute-start | bytes 196616 | tf_op jit(solution)/shard_map/ppermute | solution.py:703
  16.4 464.8 %reduce-scatter.7.cloned.1.call-start = ((), (), s32[]{:S(2)}) async-start(), calls=%async_computation.6 | async-start | bytes 1824768
  23.5 45.0 %copy-start.71 = (bf16[4,3,512]{2,0,1:T(4,128)(2,1)S(1)}, bf16[4,3,512]{2,0,1:T(4,128)(2,1)}, u32[]{:S(2)}) copy-start(bf16[4,3,512]{2,0,1:T(4,128)(2,1)} %param.31) | copy-start | bytes 36868
  68.3 76.4 %copy-start.46 = (bf16[128,1664]{1,0:T(8,128)(2,1)}, bf16[128,1664]{1,0:T(8,128)(2,1)S(1)}, u32[]{:S(2)}) copy-start(bf16[128,1664]{1,0:T(8,128)(2,1)S(1)} %reshape.279) | copy-start | bytes 1277956
  192.4 30.7 %copy-start.2 = (f32[256,512]{1,0:T(8,128)}, f32[256,512]{1,0:T(8,128)S(1)}, u32[]{:S(2)}) copy-start(f32[256,512]{1,0:T(8,128)S(1)} %get-tuple-element.60.k_ref) | copy-start | bytes 1572868
  192.5 30.8 %copy-start.73 = (f32[128]{0:T(128)S(1)}, f32[128]{0:T(128)}, u32[]{:S(2)}) copy-start(f32[128]{0:T(128)} %param.29) | copy-start | bytes 1540
  228.5 26.4 %copy-start.26 = (bf16[256,2048]{1,0:T(8,128)(2,1)S(1)}, bf16[256,2048]{1,0:T(8,128)(2,1)}, u32[]{:S(2)}) copy-start(bf16[256,2048]{1,0:T(8,128)(2,1)} %param.23) | copy-start | bytes 3145732
  279.6 52.6 %slice-start = ((s8[20971520]{0:T(1024)(128)(4,1)}), s8[4194304]{0:T(1024)(128)(4,1)S(1)}, s32[]{:S(2)}) async-start(s8[20971520]{0:T(1024)(128)(4,1)} %bitcast.158), calls=%async_computation.7 | async-start | bytes 8388608
  279.6 52.6 %slice-start.1 = ((s8[20971520]{0:T(1024)(128)(4,1)}), s8[4194304]{0:T(1024)(128)(4,1)S(1)}, s32[]{:S(2)}) async-start(s8[20971520]{0:T(1024)(128)(4,1)} %bitcast.158), calls=%async_computation.8 | async-start | bytes 8388608
  279.6 52.6 %slice-start.2 = ((s8[20971520]{0:T(1024)(128)(4,1)}), s8[4194304]{0:T(1024)(128)(4,1)S(1)}, s32[]{:S(2)}) async-start(s8[20971520]{0:T(1024)(128)(4,1)} %bitcast.158), calls=%async_computation.9 | async-start | bytes 8388608
  295.1 31.1 %copy-start.21 = (f32[256,2048]{1,0:T(8,128)S(1)}, f32[256,2048]{1,0:T(8,128)}, u32[]{:S(2)}) copy-start(f32[256,2048]{1,0:T(8,128)} %copy-done.20) | copy-start | bytes 6291460
  295.1 37.1 %slice-start.3 = ((s8[20971520]{0:T(1024)(128)(4,1)}), s8[4194304]{0:T(1024)(128)(4,1)S(1)}, s32[]{:S(2)}) async-start(s8[20971520]{0:T(1024)(128)(4,1)} %bitcast.158), calls=%async_computation.10 | async-start | bytes 8388608
  297.0 29.6 %copy-start.37 = (bf16[256,2048]{1,0:T(8,128)(2,1)S(1)}, bf16[256,2048]{1,0:T(8,128)(2,1)}, u32[]{:S(2)}) copy-start(bf16[256,2048]{1,0:T(8,128)(2,1)} %all-gather.2.cloned.1.call-done) | copy-start | bytes 3145732
  349.3 137.4 %reduce-scatter.5.cloned.1.call-start = ((), (), s32[]{:S(2)}) async-start(), calls=%async_computation.4 | async-start | bytes 1310720 | tf_op jit(solution)/shard_map/reduce_scatter | solution.py:832
  394.0 14.2 %collective-permute-start.2 = (f32[3,1536]{1,0:T(4,128)S(1)}, f32[3,1536]{1,0:T(4,128)S(1)}, u32[]{:S(2)}, u32[]{:S(2)}) collective-permute-start(f32[3,1536]{1,0:T(4,128)S(1)} %slice.341), channel_id=1, source_target_pairs={{4,0},{8,4},{12,8},{16,12},{20,16},{24,20},{28,24},{32,28},{36,32}... | collective-permute-start | bytes 55304 | tf_op jit(solution)/shard_map/ppermute | solution.py:703
  417.6 38.6 %copy-start.36 = (bf16[272,2048]{1,0:T(8,128)(2,1)S(1)}, bf16[272,2048]{1,0:T(8,128)(2,1)}, u32[]{:S(2)}) copy-start(bf16[272,2048]{1,0:T(8,128)(2,1)} %copy-done.35) | copy-start | bytes 3342340
  420.1 36.7 %copy-start.49 = (bf16[32,48,128]{2,1,0:T(8,128)(2,1)S(1)}, bf16[32,48,128]{2,1,0:T(8,128)(2,1)}, u32[]{:S(2)}) copy-start(bf16[32,48,128]{2,1,0:T(8,128)(2,1)} %reshape_reshape.16) | copy-start | bytes 1179652
  458.0 20.6 %all-to-all-start = ((bf16[32,116,128]{2,1,0:T(8,128)(2,1)}), bf16[32,116,128]{2,1,0:T(8,128)(2,1)}, u32[]{:S(2)}, u32[]{:S(2)}) async-start(bf16[32,116,128]{2,1,0:T(8,128)(2,1)} %fusion.71), calls=%async_computation.1 | async-start | bytes 1966080 | tf_op jit(solution)/shard_map/all_to_all | solution.py:910
  463.3 30.6 %copy-start.1 = (bf16[16,6,128]{2,0,1:T(8,128)(2,1)S(1)}, bf16[16,6,128]{2,0,1:T(8,128)(2,1)}, u32[]{:S(2)}) copy-start(bf16[16,6,128]{2,0,1:T(8,128)(2,1)} %param.37) | copy-start | bytes 73732
  482.6 10.1 %all-to-all-start.1 = ((f32[4,2,16,128]{3,2,1,0:T(8,128)}), f32[4,2,16,128]{3,2,1,0:T(8,128)S(1)}, u32[]{:S(2)}, u32[]{:S(2)}) async-start(f32[4,2,16,128]{3,2,1,0:T(8,128)} %pad_maximum_fusion.5), calls=%async_computation.2 | async-start | bytes 131072 | tf_op jit(solution)/shard_map/all_to_all | solution.py:912
  (68 other events, 347.4 us)
Sparse Core Ops, SparseCore 0:
  16.5 25.6 all-gather.1
  349.4 72.5 reduce-scatter.6
  424.5 33.9 reduce-scatter.4
